TPU v7x, 32 devices: a whole 2x2x4 slice. The times are simulated.
32 devices in a mesh: seq: 16 (over z, x, core), tp: 2 (over y).
Axes of the slice: x: 2, y: 2, z: 4, core: 2. Of those that a mesh axis runs over, the one named last changes fastest.
Arguments:
- trunk: bfloat16 [2048, 4096], P('seq', 'tp')
- trunk_gain: bfloat16 [4096], P('tp'), may hold values from 0.25 to 1.75
- w_in: bfloat16 [8, 1024, 4096], P('tp'), may hold values from -0.09375 to 0.09375
- depth_gain: bfloat16 [1024], replicated, may hold values from 0.25 to 1.75
- w_qkv: bfloat16 [8, 3072, 1024], P('tp', 'seq')
- w_out: bfloat16 [8, 1024, 1024], P('tp', 'seq'), may hold values from -0.1875 to 0.1875
- text_table: bfloat16 [16000, 1024], P(None, 'seq'), may hold values from -6 to 6
- audio_table: bfloat16 [7, 2048, 1024], P(None, None, 'seq'), may hold values from -6 to 6
- text_ids: int32 [2048], replicated, may hold values from 0 to 15999
- audio_ids: int32 [2048, 7], replicated, may hold values from 0 to 2047
- depth_cot: bfloat16 [8, 2048, 1024], P('tp', 'seq'), may hold values from -6 to 6
Outputs:
- depth_out: bfloat16 [8, 2048, 1024], P('tp', 'seq')
- trunk_grad: bfloat16 [2048, 4096], P('seq', 'tp')
- qkv_grad: float32 [8, 3072, 1024], P('tp', 'seq')
- out_grad: float32 [8, 1024, 1024], P('tp', 'seq')
All inputs are finite; a program needn't handle non-finite values.
Results may differ from a plain program's by a relative error of at most 0.028.
The roundings to bfloat16 on the way count: a program that leaves them out, or rounds other values in their place, can miss the bound.
Values may be sent and summed in bfloat16 or wider, within the bound.
A program may use at most 192 MiB of HBM per device.

v0:
```python
import math

import jax
import jax.numpy as jnp
from jax import lax
from jax.sharding import PartitionSpec as P

DEPTH_DIM = 1024
HEADS = 16
HEAD_DIM = 64


EPSILON = 1e-05


def inverse_rms(values):
    return lax.rsqrt(jnp.mean(values * values, axis=-1, keepdims=True) + EPSILON)


def causal_mask(count):
    order = jnp.arange(count)
    return order[:, None] >= order[None, :]


def softmax_rows(scores, count):
    masked = jnp.where(causal_mask(count), scores, -jnp.inf)
    highest = jnp.max(masked, axis=-1, keepdims=True)
    shifted = jnp.exp(masked - highest)
    return shifted / jnp.sum(shifted, axis=-1, keepdims=True)


def to_timesteps(values):
    return lax.all_to_all(values, "tp", split_axis=1, concat_axis=0, tiled=True)


def to_codebooks(values):
    return lax.all_to_all(values, "tp", split_axis=0, concat_axis=1, tiled=True)


def local(
    trunk,
    trunk_gain,
    w_in,
    depth_gain,
    w_qkv,
    w_out,
    text_table,
    audio_table,
    text_ids,
    audio_ids,
    depth_cot,
):
    model_width = trunk.shape[1] * lax.axis_size("tp")
    local_books = w_in.shape[0]
    trunk_float = trunk.astype(jnp.float32)
    gain_local = trunk_gain.astype(jnp.float32)
    whole_rows, whole_gain = (
        lax.all_gather(trunk, "tp", axis=1, tiled=True),
        lax.all_gather(trunk_gain.reshape(1, -1), "tp", axis=1, tiled=True),
    )
    whole_float = whole_rows.astype(jnp.float32)
    row_scale = inverse_rms(whole_float)
    normed = (whole_float * row_scale * whole_gain.astype(jnp.float32)).astype(jnp.bfloat16)
    first_book = lax.axis_index("tp") * local_books
    text_rows = jnp.take(text_table, text_ids, axis=0)
    columns = []
    for offset in range(local_books):
        book_index = first_book + offset
        earlier = jnp.maximum(book_index - 1, 0)
        table = lax.dynamic_index_in_dim(audio_table, earlier, 0, keepdims=False)
        tokens = lax.dynamic_index_in_dim(audio_ids, earlier, 1, keepdims=False)
        columns.append(jnp.where(book_index == 0, text_rows, jnp.take(table, tokens, axis=0)))
    embedded = lax.all_to_all(jnp.stack(columns), "seq", split_axis=1, concat_axis=2, tiled=True)
    hidden = jnp.einsum(
        "td,cjd->ctj", normed, w_in, preferred_element_type=jnp.float32
    ) + embedded.astype(jnp.float32)
    depth_scale = inverse_rms(hidden)
    depth_weight = depth_gain.astype(jnp.float32)
    depth_normed = (hidden * depth_scale * depth_weight).astype(jnp.bfloat16)
    qkv_full, out_full = (
        lax.all_gather(w_qkv, "seq", axis=1, tiled=True),
        lax.all_gather(w_out, "seq", axis=1, tiled=True),
    )
    projected = jnp.einsum(
        "ctm,cjm->ctj", depth_normed, qkv_full, preferred_element_type=jnp.float32
    ).astype(jnp.bfloat16)
    timed = to_timesteps(projected)
    books, steps_here = (timed.shape[0], timed.shape[1])
    parts = timed.reshape(books, steps_here, 3, HEADS, HEAD_DIM)
    query, keys, values = (parts[:, :, 0], parts[:, :, 1], parts[:, :, 2])
    root = math.sqrt(HEAD_DIM)
    scores = jnp.einsum("ithd,jthd->thij", query, keys, preferred_element_type=jnp.float32) / root
    probs = softmax_rows(scores, books)
    weights_low = probs.astype(jnp.bfloat16)
    attended_time = jnp.einsum(
        "thij,jthd->ithd", weights_low, values, preferred_element_type=jnp.float32
    ).astype(jnp.bfloat16)
    attended = to_codebooks(attended_time.reshape(books, steps_here, DEPTH_DIM))
    out_terms = jnp.einsum("ctm,cjm->ctj", attended, out_full, preferred_element_type=jnp.float32)
    depth_out = (hidden + out_terms).astype(jnp.bfloat16)
    out_term = jnp.einsum("ctj,cti->cji", depth_cot, attended, preferred_element_type=jnp.float32)
    qkv_back, out_back = (
        lax.all_gather(w_qkv, "seq", axis=1, tiled=True),
        lax.all_gather(w_out, "seq", axis=1, tiled=True),
    )
    d_attended = jnp.einsum(
        "ctj,cji->cti", depth_cot, out_back, preferred_element_type=jnp.float32
    ).astype(jnp.bfloat16)
    d_time = to_timesteps(d_attended).reshape(books, steps_here, HEADS, HEAD_DIM)
    d_weights = jnp.einsum("ithd,jthd->thij", d_time, values, preferred_element_type=jnp.float32)
    d_values = jnp.einsum(
        "thij,ithd->jthd", weights_low, d_time, preferred_element_type=jnp.float32
    )
    d_scores = probs * (d_weights - jnp.sum(probs * d_weights, axis=-1, keepdims=True))
    d_query = jnp.einsum("thij,jthd->ithd", d_scores, keys.astype(jnp.float32)) / root
    d_keys = jnp.einsum("thij,ithd->jthd", d_scores, query.astype(jnp.float32)) / root
    d_joined = jnp.stack([d_query, d_keys, d_values], axis=2).astype(jnp.bfloat16)
    d_projected = to_codebooks(d_joined.reshape(books, steps_here, 3 * DEPTH_DIM))
    qkv_term = jnp.einsum(
        "ctj,cti->cji", d_projected, depth_normed, preferred_element_type=jnp.float32
    )
    qkv_grad, out_grad = (
        lax.psum_scatter(
            qkv_term.astype(jnp.bfloat16), "seq", scatter_dimension=1, tiled=True
        ).astype(jnp.float32),
        lax.psum_scatter(
            out_term.astype(jnp.bfloat16), "seq", scatter_dimension=1, tiled=True
        ).astype(jnp.float32),
    )
    d_normed = jnp.einsum("ctj,cjm->ctm", d_projected, qkv_back, preferred_element_type=jnp.float32)
    gained = depth_weight * d_normed
    d_hidden = depth_cot.astype(jnp.float32) + depth_scale * gained
    d_hidden = d_hidden - hidden * depth_scale**3 * jnp.mean(
        hidden * gained, axis=-1, keepdims=True
    )
    d_hidden = d_hidden.astype(jnp.bfloat16)
    d_partial = jnp.einsum("ctj,cjd->td", d_hidden, w_in, preferred_element_type=jnp.float32)
    d_features = lax.psum_scatter(
        d_partial.astype(jnp.bfloat16), "tp", scatter_dimension=1, tiled=True
    ).astype(jnp.float32)
    trunk_gained = gain_local * d_features
    row_total = lax.psum(jnp.sum(trunk_float * trunk_gained, axis=1, keepdims=True), "tp")
    trunk_grad = row_scale * trunk_gained - trunk_float * row_scale**3 * row_total / model_width
    return (depth_out, trunk_grad.astype(jnp.bfloat16), qkv_grad, out_grad)


def solution(mesh):
    in_specs = (
        P("seq", "tp"),
        P("tp"),
        P("tp", None, None),
        P(),
        P("tp", "seq", None),
        P("tp", "seq", None),
        P(None, "seq"),
        P(None, None, "seq"),
        P(),
        P(),
        P("tp", "seq", None),
    )
    out_specs = (P("tp", "seq", None), P("seq", "tp"), P("tp", "seq", None), P("tp", "seq", None))
    return jax.shard_map(local, mesh=mesh, in_specs=in_specs, out_specs=out_specs, check_vma=False)
```

profile of v0, /device:TPU:11, one launch (start us, length us, event | category | flops | bytes accessed | tf_op | source)
XLA Modules:
  0.0 935.9 jit_solution(155997798620683525)
XLA Ops:
  11.0 4.8 copy.103
  16.7 6.2 gather_fusion.1
  22.9 8.3 gather_fusion
  31.2 6.2 gather_fusion.2
  37.4 6.2 gather_fusion.3
  43.6 6.2 gather_fusion.4
  49.9 2.2 fusion.33
  52.7 9.8 %copy.165 = bf16[4,2048,64]{2,0,1:T(4,128)(2,1)S(1)} copy(bf16[4,2048,64]{2,1,0:T(8,128)(2,1)S(1)} %pad_maximum_fusion.1) | data formatting | bytes 2097152 | tf_op jit(solution)/shard_map/stack | solution.py:73
  62.5 2.2 reshape.143
  64.7 6.6 all-to-all-start
  71.3 3.7 all-gather
  76.5 46.4 %all-to-all-done = bf16[16,2,16384]{2,1,0:T(2,128)(2,1)S(1)} async-done(((bf16[16,2,16384]{2,1,0:T(2,128)(2,1)}), bf16[16,2,16384]{2,1,0:T(2,128)(2,1)S(1)}, u32[]{:S(2)}, u32[]{:S(2)}) %all-to-all-start) | async-done | bytes 1048608 | tf_op jit(solution)/shard_map/all_to_all | solution.py:73
  128.6 17.3 %multiply_reduce_fusion.2 = (f32[4,128]{1,0:T(4,128)S(1)}, f32[4,128,1024]{2,1,0:T(8,128)S(1)}) fusion(f32[4,128,1024]{2,1,0:T(8,128)} %copy.111, bf16[4,1024,4096]{2,1,0:T(8,128)(2,1)} %param.15, bf16[128,4096]{1,0:T(8,128)(2,1)} %all-gather.5.cloned.1.call-done, f32[4096]{0:T(1024)S(1)} %mul.153, f32[128]{0:T(128)S(1)} %get-tuple-element.43), kind=kOutput, calls=%fused_computation.39 | convolution fusion | flops 4298636800 | bytes 38816256 | tf_op jit(solution)/shard_map/td,cjd->ctj/dot_general | solution.py:74
  146.0 4.9 convolution_convert_fusion.2
  152.7 4.5 all-to-all-start.3
  157.2 101.3 %all-gather.7.cloned.1.call-done = bf16[4,3072,1024]{2,1,0:T(8,128)(2,1)} async-done(((bf16[4,192,1024]{2,1,0:T(8,128)(2,1)}), bf16[4,3072,1024]{2,1,0:T(8,128)(2,1)}) %all-gather.7.cloned.1.call-update) | async-done | bytes 25165840 | tf_op jit(solution)/shard_map/all_gather | solution.py:81
  258.4 14.1 %convolution_convert_fusion.1 = bf16[4,128,3072]{2,1,0:T(8,128)(2,1)} fusion(bf16[4,3072,1024]{2,1,0:T(8,128)(2,1)} %all-gather.7.cloned.1.call-done, f32[4,128,1024]{2,1,0:T(8,128)S(1)} %get-tuple-element.45, f32[1024]{0:T(1024)S(1)} %convert_element_type.92, f32[4,128]{1,0:T(4,128)S(1)} %get-tuple-element.41), kind=kOutput, calls=%fused_computation.11 | convolution fusion | flops 3224371200 | bytes 30414848 | tf_op jit(solution)/shard_map/ctm,cjm->ctj/dot_general | solution.py:84
  272.6 6.0 copy.112
  278.6 5.2 all-to-all-start.1
  284.2 2.5 copy.164
  286.7 4.0 reshape.79
  290.8 29.0 %all-to-all-done.1 = bf16[4,128,3072]{2,0,1:T(4,128)(2,1)} async-done(((bf16[4,128,3072]{2,0,1:T(4,128)(2,1)}), bf16[4,128,3072]{2,0,1:T(4,128)(2,1)}, u32[]{:S(2)}, u32[]{:S(2)}) %all-to-all-start.1) | async-done | bytes 3145760 | tf_op jit(solution)/shard_map/all_to_all | solution.py:33
  319.8 4.5 copy.163
  324.3 8.5 reshape.77
  332.8 4.0 fusion.41
  336.8 2.5 fusion.10
  339.4 15.9 %fusion.42 = (f32[64,16,8]{2,1,0:T(8,128)S(1)}, f32[64,16,8,8]{2,3,1,0:T(8,128)S(1)}) fusion(f32[64,16,8,8]{2,3,1,0:T(8,128)S(1)} %fusion.10, pred[8,8]{0,1:T(8,128)(4,1)S(1)} %iota_compare_fusion), kind=kOutput, calls=%fused_computation.108 | output fusion | flops 393223 | bytes 557120 | tf_op jit(solution)/shard_map/sub | solution.py:28
  355.3 1.9 convert_bitcast_fusion.1
  357.3 5.1 multiply_reduce_fusion
  362.4 4.6 fusion.14
  367.0 4.8 fusion.13
  373.5 3.6 copy.125
  377.2 8.7 convert_element_type.102
  385.9 39.0 %all_to_all.75 = bf16[8,64,3072]{2,1,0:T(8,128)(2,1)S(1)} all-to-all(bf16[8,64,3072]{2,1,0:T(8,128)(2,1)} %convert_element_type.102), channel_id=1, replica_groups=mesh['seq'=16,'tp'=2] {'tp'}, dimensions={0} | all-to-all | bytes 6291456 | tf_op jit(solution)/shard_map/all_to_all | solution.py:37
  425.1 14.2 %multiply_reduce_fusion.1 = (f32[4,128]{1,0:T(4,128)S(1)}, f32[4,128,1024]{2,1,0:T(8,128)}) fusion(f32[4,128,1024]{2,1,0:T(8,128)S(1)} %get-tuple-element.45, f32[1024]{0:T(1024)S(1)} %convert_element_type.92, bf16[4,128,3072]{2,1,0:T(8,128)(2,1)S(1)} %bitcast.115, bf16[4,3072,1024]{2,1,0:T(8,128)(2,1)} %all-gather.7.cloned.1.call-done), kind=kOutput, calls=%fused_computation.31 | convolution fusion | flops 3222797824 | bytes 32512000 | tf_op jit(solution)/shard_map/ctj,cjm->ctm/dot_general | solution.py:130
  439.2 17.2 %fusion.1 = bf16[128,4096]{1,0:T(8,128)(2,1)} fusion(bf16[4,1024,4096]{2,1,0:T(8,128)(2,1)} %param.15, f32[4,128,1024]{2,1,0:T(8,128)S(1)} %get-tuple-element.45, bf16[4,128,1024]{2,1,0:T(8,128)(2,1)S(1)} %copy-done.1, f32[4,128,1024]{2,1,0:T(8,128)} %get-tuple-element.51, f32[4,128]{1,0:T(4,128)S(1)} %broadcast_multiply_fusion, ...), kind=kOutput, calls=%fused_computation.10 | convolution fusion | flops 4299685888 | bytes 39856128 | tf_op jit(solution)/shard_map/ctj,cjd->td/dot_general | solution.py:137
  456.5 4.1 convert_bitcast_fusion.2
  462.3 4.1 reshape.78
  466.4 20.8 %all_to_all.76 = bf16[8,64,1024]{2,1,0:T(8,128)(2,1)S(1)} all-to-all(bf16[8,64,1024]{2,1,0:T(8,128)(2,1)} %reshape.78), channel_id=1, replica_groups=mesh['seq'=16,'tp'=2] {'tp'}, dimensions={0} | all-to-all | bytes 2097152 | tf_op jit(solution)/shard_map/all_to_all | solution.py:37
  488.2 5.6 convert_bitcast_fusion
  493.8 14.9 %copy.129 = bf16[4,1024,1024]{2,0,1:T(4,128)(2,1)} copy(bf16[4,1024,1024]{1,2,0:T(8,128)(2,1)} %convert_bitcast_fusion) | data formatting | bytes 16777216 | tf_op jit(solution)/shard_map/convert_element_type | solution.py:127
  508.8 13.5 %convolution_convert_fusion = bf16[4,3072,1024]{2,1,0:T(8,128)(2,1)} fusion(bf16[4,128,3072]{2,1,0:T(8,128)(2,1)} %bitcast.116, f32[4,128,1024]{2,1,0:T(8,128)S(1)} %get-tuple-element.45, f32[1024]{0:T(1024)S(1)} %convert_element_type.92, f32[4,128]{1,0:T(4,128)S(1)} %get-tuple-element.41), kind=kOutput, calls=%fused_computation.6 | convolution fusion | flops 3235381248 | bytes 30414848 | tf_op jit(solution)/shard_map/ctj,cti->cji/dot_general | solution.py:119
  524.2 7.3 add_convert_fusion
  533.0 4.2 psum.7
  537.1 2.5 fusion.18
  539.6 139.4 %all-reduce.3.cloned.1.call-done = bf16[4,1024,1024]{2,0,1:T(4,128)(2,1)} async-done(((bf16[4,1024,1024]{2,0,1:T(4,128)(2,1)}), bf16[4,1024,1024]{2,0,1:T(4,128)(2,1)}) %all-reduce.3.cloned.1.call-update) | async-done | bytes 8388624
  681.8 243.5 %reduce-scatter.5.cloned.1.call-done = bf16[4,192,1024]{2,1,0:T(8,128)(2,1)} async-done(((bf16[4,3072,1024]{2,1,0:T(8,128)(2,1)}), bf16[4,192,1024]{2,1,0:T(8,128)(2,1)}) %reduce-scatter.5.cloned.1.call-update) | async-done | bytes 1572880 | tf_op jit(solution)/shard_map/reduce_scatter | solution.py:123
  925.3 3.5 convert_element_type.109
  (80 shorter events, 24.9 us)
Async XLA Ops:
  7.2 67.8 %all-gather.5.cloned.1.call-start = ((), (), s32[]{:S(2)}) async-start(), calls=%async_computation.7 | async-start | bytes 1572864 | tf_op jit(solution)/shard_map/all_gather | solution.py:58
  7.9 138.1 %all-gather.9.cloned.1.call-start = ((), (), s32[]{:S(2)}) async-start(), calls=%async_computation.9 | async-start | bytes 8912896 | tf_op jit(solution)/shard_map/all_gather | solution.py:82
  8.6 249.8 %all-gather.7.cloned.1.call-start = ((), (), s32[]{:S(2)}) async-start(), calls=%async_computation.8 | async-start | bytes 26738688 | tf_op jit(solution)/shard_map/all_gather | solution.py:81
  15.7 0.9 copy-start.8
  16.7 6.2 copy-start.6
  62.4 8.8 copy-start.7
  62.4 12.5 %copy-start.9 = (bf16[1024]{0:T(1024)(128)(2,1)S(1)}, bf16[1024]{0:T(1024)(128)(2,1)}, u32[]{:S(2)}) copy-start(bf16[1024]{0:T(1024)(128)(2,1)} %param.16) | copy-start | bytes 6148
  64.7 58.2 %all-to-all-start = ((bf16[16,2,16384]{2,1,0:T(2,128)(2,1)}), bf16[16,2,16384]{2,1,0:T(2,128)(2,1)S(1)}, u32[]{:S(2)}, u32[]{:S(2)}) async-start(bf16[16,2,16384]{2,1,0:T(2,128)(2,1)} %reshape.143), calls=%async_computation | async-start | bytes 2097152 | tf_op jit(solution)/shard_map/all_to_all | solution.py:73
  128.6 17.3 %copy-start.1 = (bf16[4,128,1024]{2,1,0:T(8,128)(2,1)S(1)}, bf16[4,128,1024]{2,1,0:T(8,128)(2,1)}, u32[]{:S(2)}) copy-start(bf16[4,128,1024]{2,1,0:T(8,128)(2,1)} %param.23) | copy-start | bytes 3145732
  152.7 125.9 %all-to-all-start.3 = ((bf16[4,128,1024]{2,0,1:T(4,128)(2,1)}), bf16[4,128,1024]{2,0,1:T(4,128)(2,1)}, u32[]{:S(2)}, u32[]{:S(2)}) async-start(bf16[4,128,1024]{2,0,1:T(4,128)(2,1)} %copy.120), calls=%async_computation.3 | async-start | bytes 2097152 | tf_op jit(solution)/shard_map/all_to_all | solution.py:33
  278.6 41.2 %all-to-all-start.1 = ((bf16[4,128,3072]{2,0,1:T(4,128)(2,1)}), bf16[4,128,3072]{2,0,1:T(4,128)(2,1)}, u32[]{:S(2)}, u32[]{:S(2)}) async-start(bf16[4,128,3072]{2,0,1:T(4,128)(2,1)} %copy.112), calls=%async_computation.1 | async-start | bytes 6291456 | tf_op jit(solution)/shard_map/all_to_all | solution.py:33
  283.8 247.7 %reduce-scatter.3.cloned.1.call-start = ((), (), s32[]{:S(2)}) async-start(), calls=%async_computation.10 | async-start | bytes 1572864 | tf_op jit(solution)/shard_map/reduce_scatter | solution.py:138
  336.8 20.4 %copy-start.5 = (bf16[8,64,1,16,64]{4,3,2,1,0:T(8,128)(2,1)}, bf16[8,64,1,16,64]{4,3,2,1,0:T(8,128)(2,1)S(1)}, u32[]{:S(2)}) copy-start(bf16[8,64,1,16,64]{4,3,2,1,0:T(8,128)(2,1)S(1)} %get-tuple-element.27) | copy-start | bytes 3145732
  339.4 16.0 %copy-start.4 = (bf16[8,64,16,64]{3,2,1,0:T(8,128)(2,1)S(1)}, bf16[8,64,16,64]{3,2,1,0:T(8,128)(2,1)}, u32[]{:S(2)}) copy-start(bf16[8,64,16,64]{3,2,1,0:T(8,128)(2,1)} %reshape.79) | copy-start | bytes 3145732
  355.3 7.1 copy-start.11
  355.3 11.7 %copy-start.12 = (f32[64,16,8]{2,1,0:T(8,128)}, f32[64,16,8]{2,1,0:T(8,128)S(1)}, u32[]{:S(2)}) copy-start(f32[64,16,8]{2,1,0:T(8,128)S(1)} %get-tuple-element.46) | copy-start | bytes 98308
  425.0 14.2 %copy-start = (bf16[4,2,64,3072]{3,2,1,0:T(8,128)(2,1)}, bf16[4,2,64,3072]{3,2,1,0:T(8,128)(2,1)S(1)}, u32[]{:S(2)}) copy-start(bf16[4,2,64,3072]{3,2,1,0:T(8,128)(2,1)S(1)} %copy.126) | copy-start | bytes 9437188
  456.5 222.6 %all-reduce.3.cloned.1.call-start = ((), (), s32[]{:S(2)}) async-start(), calls=%async_computation.12 | async-start | bytes 16777216
  487.2 1.0 copy-start.2
  508.7 416.6 %reduce-scatter.5.cloned.1.call-start = ((), (), s32[]{:S(2)}) async-start(), calls=%async_computation.11 | async-start | bytes 26738688 | tf_op jit(solution)/shard_map/reduce_scatter | solution.py:123
  522.3 0.7 copy-start.10
  522.3 1.9 copy-start.3
Sparse Core Ops, SparseCore 0:
  9.5 22.4 all-gather.4
  34.2 90.3 all-gather.8
  126.2 132.2 all-gather.6
  456.6 23.5 reduce-scatter.2
  508.9 170.1 all-reduce.2
  683.0 242.2 reduce-scatter.4
where the time goes:
time: 948 us; the launch traced here: 936 us
  waiting for transfers between devices  562 us (59%)
  local copies, waits for them, and re-layouts  126 us (13%)
  matrix products  117 us (12%)
  blocking collectives  67.6 us (7%)
  other arithmetic  30.9 us (3%)
  starting transfers between devices  16.9 us (2%)
  between operations  15.5 us (2%)
    reduce_scatter x1, waiting for transfers between devices, local(): lax.psum_scatter(qkv_term.astype(jnp.bfloat16), 'seq', scatter_dimension=...  244 us
    unnamed x7, waiting for transfers between devices  141 us
    all_gather x1, waiting for transfers between devices, local(): lax.all_gather(w_qkv, 'seq', axis=1, tiled=True)  101 us
    all_to_all x2, blocking collectives, to_codebooks(): return lax.all_to_all(values, 'tp', split_axis=0, concat_axis=1, tiled=True)  59.7 us
    all_to_all x1, waiting for transfers between devices, local(): lax.all_to_all(jnp.stack(columns), 'seq', split_axis=1, concat_axis=2, ti...  46.4 us
    all_to_all x2, waiting for transfers between devices, to_timesteps(): return lax.all_to_all(values, 'tp', split_axis=1, concat_axis=0, tiled=True)  29 us
    gather x4, local copies, waits for them, and re-layouts, local(): jnp.take(table, tokens, axis=0)  24.7 us
  transfers between devices with their start and end apart: 9, of which 5 were waited for; matrix products, arithmetic and copies ran while one was open for 18% of the time, Pallas kernels for 0%

commit v1 on v0

--- a/solution.py
+++ b/solution.py
@@ -77,14 +77,21 @@
     depth_scale = inverse_rms(hidden)
     depth_weight = depth_gain.astype(jnp.float32)
     depth_normed = (hidden * depth_scale * depth_weight).astype(jnp.bfloat16)
-    qkv_full, out_full = (
-        lax.all_gather(w_qkv, "seq", axis=1, tiled=True),
-        lax.all_gather(w_out, "seq", axis=1, tiled=True),
-    )
+    qkv_full = lax.all_gather(w_qkv, "seq", axis=1, tiled=True)
+    cot_here, depth_normed = lax.optimization_barrier((depth_cot, depth_normed))
+    cot_columns = lax.all_to_all(cot_here, "seq", split_axis=2, concat_axis=1, tiled=True)
+    cot_columns, depth_normed = lax.optimization_barrier((cot_columns, depth_normed))
     projected = jnp.einsum(
         "ctm,cjm->ctj", depth_normed, qkv_full, preferred_element_type=jnp.float32
     ).astype(jnp.bfloat16)
+    w_out, projected = lax.optimization_barrier((w_out, projected))
+    out_full = lax.all_gather(w_out, "seq", axis=1, tiled=True)
+    d_attended = jnp.einsum(
+        "ctj,cji->cti", depth_cot, out_full, preferred_element_type=jnp.float32
+    ).astype(jnp.bfloat16)
     timed = to_timesteps(projected)
+    rows_here, timed = lax.optimization_barrier((depth_normed, timed))
+    normed_all = lax.all_gather(rows_here, "seq", axis=1, tiled=True)
     books, steps_here = (timed.shape[0], timed.shape[1])
     parts = timed.reshape(books, steps_here, 3, HEADS, HEAD_DIM)
     query, keys, values = (parts[:, :, 0], parts[:, :, 1], parts[:, :, 2])
@@ -98,14 +105,10 @@
     attended = to_codebooks(attended_time.reshape(books, steps_here, DEPTH_DIM))
     out_terms = jnp.einsum("ctm,cjm->ctj", attended, out_full, preferred_element_type=jnp.float32)
     depth_out = (hidden + out_terms).astype(jnp.bfloat16)
-    out_term = jnp.einsum("ctj,cti->cji", depth_cot, attended, preferred_element_type=jnp.float32)
-    qkv_back, out_back = (
-        lax.all_gather(w_qkv, "seq", axis=1, tiled=True),
-        lax.all_gather(w_out, "seq", axis=1, tiled=True),
+    attended_all = lax.all_gather(attended, "seq", axis=1, tiled=True)
+    out_grad = jnp.einsum(
+        "ctj,cti->cji", cot_columns, attended_all, preferred_element_type=jnp.float32
     )
-    d_attended = jnp.einsum(
-        "ctj,cji->cti", depth_cot, out_back, preferred_element_type=jnp.float32
-    ).astype(jnp.bfloat16)
     d_time = to_timesteps(d_attended).reshape(books, steps_here, HEADS, HEAD_DIM)
     d_weights = jnp.einsum("ithd,jthd->thij", d_time, values, preferred_element_type=jnp.float32)
     d_values = jnp.einsum(
@@ -116,18 +119,12 @@
     d_keys = jnp.einsum("thij,ithd->jthd", d_scores, query.astype(jnp.float32)) / root
     d_joined = jnp.stack([d_query, d_keys, d_values], axis=2).astype(jnp.bfloat16)
     d_projected = to_codebooks(d_joined.reshape(books, steps_here, 3 * DEPTH_DIM))
-    qkv_term = jnp.einsum(
-        "ctj,cti->cji", d_projected, depth_normed, preferred_element_type=jnp.float32
+    d_projected, normed_all = lax.optimization_barrier((d_projected, normed_all))
+    d_columns = lax.all_to_all(d_projected, "seq", split_axis=2, concat_axis=1, tiled=True)
+    qkv_grad = jnp.einsum(
+        "ctj,cti->cji", d_columns, normed_all, preferred_element_type=jnp.float32
     )
-    qkv_grad, out_grad = (
-        lax.psum_scatter(
-            qkv_term.astype(jnp.bfloat16), "seq", scatter_dimension=1, tiled=True
-        ).astype(jnp.float32),
-        lax.psum_scatter(
-            out_term.astype(jnp.bfloat16), "seq", scatter_dimension=1, tiled=True
-        ).astype(jnp.float32),
-    )
-    d_normed = jnp.einsum("ctj,cjm->ctm", d_projected, qkv_back, preferred_element_type=jnp.float32)
+    d_normed = jnp.einsum("ctj,cjm->ctm", d_projected, qkv_full, preferred_element_type=jnp.float32)
     gained = depth_weight * d_normed
     d_hidden = depth_cot.astype(jnp.float32) + depth_scale * gained
     d_hidden = d_hidden - hidden * depth_scale**3 * jnp.mean(

time: 948 us -> 669 us (0.71)
  waiting for transfers between devices: 562 us -> 199 us
  blocking collectives: 67.6 us -> 159 us
    reduce_scatter x1 -> x0, waiting for transfers between devices: 244 us -> none  [local(): lax.psum_scatter(qkv_term.astype(jnp.bfloat16), 'seq', scatter_dimension=...]
    unnamed x7 -> x6, waiting for transfers between devices: 141 us -> 1.44 us
    all_to_all x0 -> x3, blocking collectives: none -> 98 us  [the longest x2 54.6 us: to_timesteps(): return lax.all_to_all(values, 'tp', split_axis=1, concat_axis=0, tiled=True)]
    all_gather x2 -> x4, waiting for transfers between devices: 101 us -> 150 us  [the longest x1 119 us: local(): attended_all = lax.all_gather(attended, 'seq', axis=1, tiled=True)]
    all_to_all x2 -> x1, waiting for transfers between devices: 29 us -> 0.01 us  [local(): lax.all_to_all(d_projected, 'seq', split_axis=2, concat_axis=1, tiled=True)]
    convert_element_type x3 -> x1, local copies, waits for them, and re-layouts: 22.7 us -> 2.64 us  [local(): d_attended = jnp.einsum('ctj,cji->cti', depth_cot, out_full, preferred_el...]
    reduce_scatter x1, waiting for transfers between devices: 0.01 us -> 16.9 us  [local(): lax.psum_scatter(d_partial.astype(jnp.bfloat16), 'tp', scatter_dimension=...]
    all_to_all x1, waiting for transfers between devices: 46.4 us -> 31.1 us  [local(): lax.all_to_all(jnp.stack(columns), 'seq', split_axis=1, concat_axis=2, ti...]
  transfers between devices with their start and end apart: 9 -> 8, of which waited for: 5 -> 4; matrix products, arithmetic and copies ran while one was open for 18% -> 37% of each run, Pallas kernels for 0% -> 0%
where the time goes in v1:
time: 669 us; the launch traced here: 658 us
  waiting for transfers between devices  199 us (30%)
  blocking collectives  159 us (24%)
  matrix products  124 us (19%)
  local copies, waits for them, and re-layouts  119 us (18%)
  other arithmetic  27.2 us (4%)
  starting transfers between devices  15.5 us (2%)
  between operations  15.1 us (2%)
    all_gather x1, waiting for transfers between devices, local(): attended_all = lax.all_gather(attended, 'seq', axis=1, tiled=True)  119 us
    all_to_all x2, blocking collectives, to_timesteps(): return lax.all_to_all(values, 'tp', split_axis=1, concat_axis=0, tiled=True)  54.6 us
    all_to_all x2, blocking collectives, to_codebooks(): return lax.all_to_all(values, 'tp', split_axis=0, concat_axis=1, tiled=True)  53 us
    all_to_all x1, blocking collectives, local(): lax.all_to_all(cot_here, 'seq', split_axis=2, concat_axis=1, tiled=True)  43.4 us
    all_to_all x1, waiting for transfers between devices, local(): lax.all_to_all(jnp.stack(columns), 'seq', split_axis=1, concat_axis=2, ti...  31.1 us
    all_gather x1, waiting for transfers between devices, local(): qkv_full = lax.all_gather(w_qkv, 'seq', axis=1, tiled=True)  30.6 us
    gather x4, local copies, waits for them, and re-layouts, local(): jnp.take(table, tokens, axis=0)  24.7 us
    dot_general x1, matrix products, local(): jnp.einsum('ctj,cjd->td', d_hidden, w_in, preferred_element_type=jnp.floa...  17.4 us
  transfers between devices with their start and end apart: 8, of which 4 were waited for; matrix products, arithmetic and copies ran while one was open for 37% of the time, Pallas kernels for 0%

profile of v1, /device:TPU:11, one launch (start us, length us, event | category | flops | bytes accessed | tf_op | source)
XLA Modules:
  0.0 657.8 jit_solution(13887149550608188598)
XLA Ops:
  10.2 4.9 copy.133
  16.0 6.2 gather_fusion.1
  22.2 8.3 %gather_fusion = bf16[2048,64]{1,0:T(8,128)(2,1)S(1)} fusion(bf16[16000,64]{1,0:T(8,128)(2,1)} %copy.133, s32[2048]{0:T(1024)S(1)} %fusion.38), kind=kCustom, calls=%fused_computation.4 | custom fusion | bytes 532480 | tf_op jit(solution)/shard_map/jit(_take)/gather | solution.py:65
  30.5 6.2 gather_fusion.2
  36.7 6.2 gather_fusion.3
  42.9 6.2 gather_fusion.4
  49.2 2.2 fusion.37
  52.0 9.8 %copy.201 = bf16[4,2048,64]{2,0,1:T(4,128)(2,1)S(1)} copy(bf16[4,2048,64]{2,1,0:T(8,128)(2,1)S(1)} %pad_maximum_fusion.1) | data formatting | bytes 2097152 | tf_op jit(solution)/shard_map/stack | solution.py:73
  61.8 2.2 reshape.141
  64.0 6.6 all-to-all-start
  70.6 3.7 all-gather
  75.9 31.1 %all-to-all-done = bf16[16,2,16384]{2,1,0:T(2,128)(2,1)S(1)} async-done(((bf16[16,2,16384]{2,1,0:T(2,128)(2,1)}), bf16[16,2,16384]{2,1,0:T(2,128)(2,1)S(1)}, u32[]{:S(2)}, u32[]{:S(2)}) %all-to-all-start) | async-done | bytes 1048608 | tf_op jit(solution)/shard_map/all_to_all | solution.py:73
  112.7 17.3 %multiply_reduce_fusion.2 = (f32[4,128]{1,0:T(4,128)S(1)}, f32[4,128,1024]{2,1,0:T(8,128)S(1)}) fusion(f32[4,128,1024]{2,1,0:T(8,128)} %copy.141, bf16[4,1024,4096]{2,1,0:T(8,128)(2,1)} %param.15, bf16[128,4096]{1,0:T(8,128)(2,1)S(1)} %copy-done.7, f32[4096]{0:T(1024)S(1)} %mul.153, f32[128]{0:T(128)S(1)} %get-tuple-element.43), kind=kOutput, calls=%fused_computation.39 | convolution fusion | flops 4298636800 | bytes 38816256 | tf_op jit(solution)/shard_map/td,cjd->ctj/dot_general | solution.py:74
  132.8 43.4 %all_to_all.114 = bf16[4,128,1024]{1,0,2:T(4,128)(2,1)S(1)} all-to-all(bf16[4,128,1024]{1,0,2:T(4,128)(2,1)} %copy.142), channel_id=1, replica_groups=mesh['seq'=16,'tp'=2] {'seq'}, dimensions={2} | all-to-all | bytes 2097152 | tf_op jit(solution)/shard_map/all_to_all | solution.py:82
  176.6 30.6 %all-gather.9.cloned.1.call-done = bf16[4,3072,1024]{2,1,0:T(8,128)(2,1)} async-done(((bf16[4,192,1024]{2,1,0:T(8,128)(2,1)}), bf16[4,3072,1024]{2,1,0:T(8,128)(2,1)}) %all-gather.9.cloned.1.call-update) | async-done | bytes 25165840 | tf_op jit(solution)/shard_map/all_gather | solution.py:80
  207.3 14.6 %convolution_convert_fusion = bf16[4,128,3072]{2,1,0:T(8,128)(2,1)} fusion(bf16[4,128,1024]{2,1,0:T(8,128)(2,1)} %multiply_convert_fusion.2, bf16[4,3072,1024]{2,1,0:T(8,128)(2,1)} %all-gather.9.cloned.1.call-done), kind=kOutput, calls=%fused_computation.9 | convolution fusion | flops 3222798336 | bytes 29360128 | tf_op jit(solution)/shard_map/ctm,cjm->ctj/dot_general | solution.py:84
  222.0 4.3 copy.145
  226.3 39.1 %all_to_all.115 = bf16[4,128,3072]{2,0,1:T(4,128)(2,1)S(1)} all-to-all(bf16[4,128,3072]{2,0,1:T(4,128)(2,1)S(1)} %copy.145), channel_id=1, replica_groups=mesh['seq'=16,'tp'=2] {'tp'}, dimensions={1} | all-to-all | bytes 6291456 | tf_op jit(solution)/shard_map/all_to_all | solution.py:33
  268.3 8.6 %reshape.76 = bf16[8,64,3,16,64]{4,3,2,1,0:T(8,128)(2,1)} reshape(bf16[8,64,3072]{2,1,0:T(8,128)(2,1)} %bitcast.131) | data formatting | bytes 6291456 | tf_op jit(solution)/shard_map/reshape | solution.py:96
  276.9 4.5 fusion.45
  281.4 2.5 fusion.13
  284.0 15.9 %fusion.46 = (f32[64,16,8]{2,1,0:T(8,128)S(1)}, f32[64,16,8,8]{2,3,1,0:T(8,128)S(1)}) fusion(f32[64,16,8,8]{2,3,1,0:T(8,128)S(1)} %fusion.13, pred[8,8]{0,1:T(8,128)(4,1)S(1)} %iota_compare_fusion), kind=kOutput, calls=%fused_computation.108 | output fusion | flops 393223 | bytes 557120 | tf_op jit(solution)/shard_map/sub | solution.py:28
  299.9 1.9 convert_bitcast_fusion.1
  303.7 4.2 reshape.77
  308.0 16.2 %all_to_all.116 = bf16[8,64,1024]{2,1,0:T(8,128)(2,1)S(1)} all-to-all(bf16[8,64,1024]{2,1,0:T(8,128)(2,1)} %reshape.77), channel_id=1, replica_groups=mesh['seq'=16,'tp'=2] {'tp'}, dimensions={0} | all-to-all | bytes 2097152 | tf_op jit(solution)/shard_map/all_to_all | solution.py:37
  325.4 7.6 %fusion.18 = bf16[4,128,1024]{1,2,0:T(8,128)(2,1)} fusion(bf16[4,1024,1024]{2,1,0:T(8,128)(2,1)} %all-gather.11.cloned.1.call-done, bf16[4,128,1024]{2,1,0:T(8,128)(2,1)} %param.23), kind=kOutput, calls=%fused_computation.48 | convolution fusion | flops 1074266112 | bytes 10485760 | tf_op jit(solution)/shard_map/ctj,cji->cti/dot_general | solution.py:89
  332.9 2.6 copy.154
  335.6 15.5 %all_to_all.117 = bf16[4,128,1024]{2,0,1:T(4,128)(2,1)S(1)} all-to-all(bf16[4,128,1024]{2,0,1:T(4,128)(2,1)} %copy.154), channel_id=1, replica_groups=mesh['seq'=16,'tp'=2] {'tp'}, dimensions={1} | all-to-all | bytes 2097152 | tf_op jit(solution)/shard_map/all_to_all | solution.py:33
  352.5 4.0 reshape.78
  356.5 4.9 convert_bitcast_fusion
  362.1 4.9 multiply_reduce_fusion
  367.1 4.7 fusion.17
  371.8 4.9 fusion.16
  378.5 3.7 copy.160
  382.2 8.7 %convert_element_type.91 = bf16[8,64,3072]{2,1,0:T(8,128)(2,1)} reshape(bf16[8,64,3,16,64]{4,3,2,1,0:T(8,128)(2,1)} %copy.160) | data formatting | bytes 6291456 | tf_op jit(solution)/shard_map/convert_element_type | solution.py:120
  390.9 36.9 %all_to_all.118 = bf16[8,64,3072]{2,1,0:T(8,128)(2,1)S(1)} all-to-all(bf16[8,64,3072]{2,1,0:T(8,128)(2,1)} %convert_element_type.91), channel_id=1, replica_groups=mesh['seq'=16,'tp'=2] {'tp'}, dimensions={0} | all-to-all | bytes 6291456 | tf_op jit(solution)/shard_map/all_to_all | solution.py:37
  429.7 6.0 copy.162
  435.7 8.5 %all-to-all-start.6 = ((bf16[4,128,3072]{1,0,2:T(4,128)(2,1)}), bf16[4,128,3072]{1,0,2:T(4,128)(2,1)}, u32[]{:S(2)}, u32[]{:S(2)}) async-start(bf16[4,128,3072]{1,0,2:T(4,128)(2,1)} %copy.162), calls=%async_computation.7 | async-start | bytes 6291456 | tf_op jit(solution)/shard_map/all_to_all | solution.py:123
  444.4 14.2 %multiply_reduce_fusion.1 = (f32[4,128]{1,0:T(4,128)S(1)}, f32[4,128,1024]{2,1,0:T(8,128)}) fusion(f32[4,128,1024]{2,1,0:T(8,128)S(1)} %get-tuple-element.45, f32[1024]{0:T(1024)S(1)} %convert_element_type.80, bf16[4,128,3072]{2,1,0:T(8,128)(2,1)} %bitcast.127, bf16[4,3072,1024]{2,1,0:T(8,128)(2,1)} %all-gather.9.cloned.1.call-done), kind=kOutput, calls=%fused_computation.31 | convolution fusion | flops 3222797824 | bytes 32512000 | tf_op jit(solution)/shard_map/ctj,cjm->ctm/dot_general | solution.py:127
  458.6 17.4 %fusion.1 = bf16[128,4096]{1,0:T(8,128)(2,1)} fusion(bf16[4,1024,4096]{2,1,0:T(8,128)(2,1)} %param.15, f32[4,128,1024]{2,1,0:T(8,128)S(1)} %get-tuple-element.45, bf16[4,128,1024]{2,1,0:T(8,128)(2,1)S(1)} %copy-done.6, f32[4,128,1024]{2,1,0:T(8,128)} %get-tuple-element.51, f32[4,128]{1,0:T(4,128)S(1)} %broadcast_multiply_fusion, ...), kind=kOutput, calls=%fused_computation.8 | convolution fusion | flops 4299685888 | bytes 39856128 | tf_op jit(solution)/shard_map/ctj,cjd->td/dot_general | solution.py:134
  476.0 7.6 %add_convert_fusion = bf16[4,128,1024]{2,1,0:T(8,128)(2,1)} fusion(f32[4,128,1024]{2,1,0:T(8,128)S(1)} %get-tuple-element.45, bf16[4,128,1024]{2,1,0:T(8,128)(2,1)} %bitcast.134, bf16[4,1024,1024]{2,1,0:T(8,128)(2,1)} %all-gather.11.cloned.1.call-done), kind=kOutput, calls=%fused_computation.33 | convolution fusion | flops 1074790400 | bytes 12582912 | tf_op jit(solution)/shard_map/ctm,cjm->ctj/dot_general | solution.py:106
  483.6 119.2 %all-gather.15.cloned.1.call-done = bf16[4,2048,1024]{2,1,0:T(8,128)(2,1)} async-done(((bf16[4,128,1024]{2,1,0:T(8,128)(2,1)}), bf16[4,2048,1024]{2,1,0:T(8,128)(2,1)}) %all-gather.15.cloned.1.call-update) | async-done | bytes 16777232 | tf_op jit(solution)/shard_map/all_gather | solution.py:108
  602.9 10.0 %fusion.47 = f32[4,64,1024]{2,1,0:T(8,128)} fusion(bf16[4,2048,64]{1,2,0:T(8,128)(2,1)S(1)} %bitcast.128, bf16[4,2048,1024]{2,1,0:T(8,128)(2,1)} %all-gather.15.cloned.1.call-done), kind=kOutput, calls=%fused_computation.110 | convolution fusion | flops 1073741824 | bytes 18874368 | tf_op jit(solution)/shard_map/ctj,cti->cji/dot_general | solution.py:109
  612.9 16.9 %reduce-scatter.2.cloned.1.call-done = bf16[128,2048]{1,0:T(8,128)(2,1)} async-done(((bf16[128,4096]{1,0:T(8,128)(2,1)}), bf16[128,2048]{1,0:T(8,128)(2,1)}) %reduce-scatter.2.cloned.1.call-update) | async-done | bytes 524304 | tf_op jit(solution)/shard_map/reduce_scatter | solution.py:135
  631.1 3.8 psum.7
  634.9 2.3 fusion.22
  637.2 2.3 copy.163
  639.5 11.1 %fusion.3 = f32[4,192,1024]{2,1,0:T(8,128)} fusion(bf16[4,2048,1024]{2,1,0:T(8,128)(2,1)} %all-gather.13.cloned.1.call-done, bf16[4,16,24,8,128]{4,3,2,1,0:T(8,128)(2,1)S(1)} %bitcast.132), kind=kOutput, calls=%fused_computation.17 | convolution fusion | flops 3221225472 | bytes 23068672 | tf_op jit(solution)/shard_map/ctj,cti->cji/dot_general | solution.py:124
  (96 shorter events, 28.3 us)
Async XLA Ops:
  7.2 67.2 %all-gather.7.cloned.1.call-start = ((), (), s32[]{:S(2)}) async-start(), calls=%async_computation.8 | async-start | bytes 1572864 | tf_op jit(solution)/shard_map/all_gather | solution.py:58
  7.9 199.4 %all-gather.9.cloned.1.call-start = ((), (), s32[]{:S(2)}) async-start(), calls=%async_computation.9 | async-start | bytes 26738688 | tf_op jit(solution)/shard_map/all_gather | solution.py:80
  10.2 5.7 copy-start.13
  15.4 6.8 %copy-start.11 = (s32[2048]{0:T(1024)S(1)}, s32[2048]{0:T(1024)}, u32[]{:S(2)}) copy-start(s32[2048]{0:T(1024)} %param.21) | copy-start | bytes 24580
  61.8 8.9 %copy-start.12 = (bf16[2048]{0:T(1024)(128)(2,1)S(1)}, bf16[2048]{0:T(1024)(128)(2,1)}, u32[]{:S(2)}) copy-start(bf16[2048]{0:T(1024)(128)(2,1)} %param.14) | copy-start | bytes 12292
  61.8 12.6 %copy-start.14 = (bf16[1024]{0:T(1024)(128)(2,1)S(1)}, bf16[1024]{0:T(1024)(128)(2,1)}, u32[]{:S(2)}) copy-start(bf16[1024]{0:T(1024)(128)(2,1)} %param.16) | copy-start | bytes 6148
  64.0 43.0 %all-to-all-start = ((bf16[16,2,16384]{2,1,0:T(2,128)(2,1)}), bf16[16,2,16384]{2,1,0:T(2,128)(2,1)S(1)}, u32[]{:S(2)}, u32[]{:S(2)}) async-start(bf16[16,2,16384]{2,1,0:T(2,128)(2,1)} %reshape.141), calls=%async_computation | async-start | bytes 2097152 | tf_op jit(solution)/shard_map/all_to_all | solution.py:73
  70.6 254.8 %all-gather.11.cloned.1.call-start = ((), (), s32[]{:S(2)}) async-start(), calls=%async_computation.10 | async-start | bytes 8912896 | tf_op jit(solution)/shard_map/all_gather | solution.py:88
  110.9 1.8 copy-start.7
  130.0 1.4 copy-start.5
  222.0 207.7 %all-gather.13.cloned.1.call-start = ((), (), s32[]{:S(2)}) async-start(), calls=%async_computation.11 | async-start | bytes 17825792 | tf_op jit(solution)/shard_map/all_gather | solution.py:94
  268.3 334.6 %all-gather.15.cloned.1.call-start = ((), (), s32[]{:S(2)}) async-start(), calls=%async_computation.13 | async-start | bytes 17825792 | tf_op jit(solution)/shard_map/all_gather | solution.py:108
  281.4 2.5 copy-start
  281.4 2.5 copy-start.2
  281.4 18.5 %copy-start.9 = (bf16[8,64,1,16,64]{4,3,2,1,0:T(8,128)(2,1)}, bf16[8,64,1,16,64]{4,3,2,1,0:T(8,128)(2,1)S(1)}, u32[]{:S(2)}) copy-start(bf16[8,64,1,16,64]{4,3,2,1,0:T(8,128)(2,1)S(1)} %get-tuple-element.27) | copy-start | bytes 3145732
  299.9 2.0 copy-start.15
  299.9 2.2 copy-start.17
  356.5 4.9 copy-start.8
  356.5 4.9 copy-start.10
  356.5 5.5 copy-start.16
  356.5 5.6 copy-start.18
  362.1 4.9 copy-start.3
  367.1 4.8 copy-start.1
  435.7 201.5 %all-to-all-start.6 = ((bf16[4,128,3072]{1,0,2:T(4,128)(2,1)}), bf16[4,128,3072]{1,0,2:T(4,128)(2,1)}, u32[]{:S(2)}, u32[]{:S(2)}) async-start(bf16[4,128,3072]{1,0,2:T(4,128)(2,1)} %copy.162), calls=%async_computation.7 | async-start | bytes 6291456 | tf_op jit(solution)/shard_map/all_to_all | solution.py:123
  444.1 185.6 %reduce-scatter.2.cloned.1.call-start = ((), (), s32[]{:S(2)}) async-start(), calls=%async_computation.12 | async-start | bytes 1572864 | tf_op jit(solution)/shard_map/reduce_scatter | solution.py:135
  444.4 14.2 %copy-start.6 = (bf16[4,128,1024]{2,1,0:T(8,128)(2,1)S(1)}, bf16[4,128,1024]{2,1,0:T(8,128)(2,1)}, u32[]{:S(2)}) copy-start(bf16[4,128,1024]{2,1,0:T(8,128)(2,1)} %param.23) | copy-start | bytes 3145732
  483.6 146.2 %copy-start.4 = (bf16[128,2048]{1,0:T(8,128)(2,1)S(1)}, bf16[128,2048]{1,0:T(8,128)(2,1)}, u32[]{:S(2)}) copy-start(bf16[128,2048]{1,0:T(8,128)(2,1)} %param.13) | copy-start | bytes 1572868
Sparse Core Ops, SparseCore 0:
  9.5 22.4 all-gather.6
  33.6 173.6 all-gather.8
  222.1 72.7 all-gather.10
  297.4 123.8 all-gather.12
  423.3 179.4 all-gather.14
  605.5 24.2 reduce-scatter.1

commit v2 on v1

--- a/solution.py
+++ b/solution.py
@@ -78,9 +78,6 @@
     depth_weight = depth_gain.astype(jnp.float32)
     depth_normed = (hidden * depth_scale * depth_weight).astype(jnp.bfloat16)
     qkv_full = lax.all_gather(w_qkv, "seq", axis=1, tiled=True)
-    cot_here, depth_normed = lax.optimization_barrier((depth_cot, depth_normed))
-    cot_columns = lax.all_to_all(cot_here, "seq", split_axis=2, concat_axis=1, tiled=True)
-    cot_columns, depth_normed = lax.optimization_barrier((cot_columns, depth_normed))
     projected = jnp.einsum(
         "ctm,cjm->ctj", depth_normed, qkv_full, preferred_element_type=jnp.float32
     ).astype(jnp.bfloat16)
@@ -105,9 +102,21 @@
     attended = to_codebooks(attended_time.reshape(books, steps_here, DEPTH_DIM))
     out_terms = jnp.einsum("ctm,cjm->ctj", attended, out_full, preferred_element_type=jnp.float32)
     depth_out = (hidden + out_terms).astype(jnp.bfloat16)
-    attended_all = lax.all_gather(attended, "seq", axis=1, tiled=True)
-    out_grad = jnp.einsum(
-        "ctj,cti->cji", cot_columns, attended_all, preferred_element_type=jnp.float32
+    indices = lax.axis_size("seq")
+    near = 2 if indices % 2 == 0 else 1
+    far = indices // near
+    pairs = [[near * k + i for i in range(near)] for k in range(far)]
+    strides = [[near * k + i for k in range(far)] for i in range(near)]
+    cot_split = depth_cot.reshape(local_books, depth_cot.shape[1], far, near, -1)
+    out_term = jnp.einsum(
+        "ctfnj,cti->nfcji", cot_split, attended, preferred_element_type=jnp.float32
+    ).astype(jnp.bfloat16)
+    out_term = lax.all_to_all(
+        out_term, "seq", split_axis=0, concat_axis=0, axis_index_groups=pairs, tiled=True
+    )
+    out_term = jnp.sum(out_term.astype(jnp.float32), axis=0).astype(jnp.bfloat16)
+    out_sum = lax.psum_scatter(
+        out_term, "seq", scatter_dimension=0, axis_index_groups=strides, tiled=False
     )
     d_time = to_timesteps(d_attended).reshape(books, steps_here, HEADS, HEAD_DIM)
     d_weights = jnp.einsum("ithd,jthd->thij", d_time, values, preferred_element_type=jnp.float32)
@@ -132,13 +141,17 @@
     )
     d_hidden = d_hidden.astype(jnp.bfloat16)
     d_partial = jnp.einsum("ctj,cjd->td", d_hidden, w_in, preferred_element_type=jnp.float32)
-    d_features = lax.psum_scatter(
-        d_partial.astype(jnp.bfloat16), "tp", scatter_dimension=1, tiled=True
-    ).astype(jnp.float32)
+    sides = lax.axis_size("tp")
+    d_pieces = d_partial.astype(jnp.bfloat16).reshape(trunk.shape[0], sides, -1)
+    d_pieces = lax.all_to_all(d_pieces, "tp", split_axis=1, concat_axis=1, tiled=True)
+    d_features = jnp.sum(d_pieces.astype(jnp.float32), axis=1)
     trunk_gained = gain_local * d_features
     row_total = lax.psum(jnp.sum(trunk_float * trunk_gained, axis=1, keepdims=True), "tp")
     trunk_grad = row_scale * trunk_gained - trunk_float * row_scale**3 * row_total / model_width
-    return (depth_out, trunk_grad.astype(jnp.bfloat16), qkv_grad, out_grad)
+    trunk_grad = trunk_grad.astype(jnp.bfloat16)
+    out_sum, trunk_grad, qkv_grad = lax.optimization_barrier((out_sum, trunk_grad, qkv_grad))
+    out_grad = out_sum.astype(jnp.float32)
+    return (depth_out, trunk_grad, qkv_grad, out_grad)
 
 
 def solution(mesh):

time: 669 us -> 734 us (1.097)
  waiting for transfers between devices: 199 us -> 326 us
  blocking collectives: 159 us -> 46.6 us
  starting transfers between devices: 15.5 us -> 40.7 us
  local copies, waits for them, and re-layouts: 119 us -> 137 us
  other arithmetic: 27.2 us -> 40.5 us
  matrix products: 124 us -> 114 us
    unnamed x6, waiting for transfers between devices: 1.44 us -> 203 us
    all_gather x1 -> x0, waiting for transfers between devices: 119 us -> none  [local(): attended_all = lax.all_gather(attended, 'seq', axis=1, tiled=True)]
    all_to_all x3 -> x0, blocking collectives: 96.5 us -> none  [the longest x2 53 us: to_codebooks(): return lax.all_to_all(values, 'tp', split_axis=0, concat_axis=1, tiled=True)]
    all_to_all x0 -> x5, waiting for transfers between devices: none -> 39 us  [the longest x2 21 us: to_codebooks(): return lax.all_to_all(values, 'tp', split_axis=0, concat_axis=1, tiled=True)]
    all_to_all x0 -> x5, starting transfers between devices: none -> 28.2 us  [the longest x2 9.87 us: to_codebooks(): return lax.all_to_all(values, 'tp', split_axis=0, concat_axis=1, tiled=True)]
    all_gather x1, waiting for transfers between devices: 30.6 us -> 54.4 us  [local(): qkv_full = lax.all_gather(w_qkv, 'seq', axis=1, tiled=True)]
    reduce_scatter x1 -> x0, waiting for transfers between devices: 16.9 us -> none  [local(): lax.psum_scatter(d_partial.astype(jnp.bfloat16), 'tp', scatter_dimension=...]
    all_to_all x2 -> x1, blocking collectives: 54.6 us -> 39.1 us  [to_timesteps(): return lax.all_to_all(values, 'tp', split_axis=1, concat_axis=0, tiled=True)]
  transfers between devices with their start and end apart: 8 -> 12, of which waited for: 4 -> 7; matrix products, arithmetic and copies ran while one was open for 37% -> 36% of each run, Pallas kernels for 0% -> 0%
where the time goes in v2:
time: 734 us; the launch traced here: 720 us
  waiting for transfers between devices  326 us (44%)
  local copies, waits for them, and re-layouts  137 us (19%)
  matrix products  114 us (16%)
  blocking collectives  46.6 us (6%)
  starting transfers between devices  40.7 us (6%)
  other arithmetic  40.5 us (6%)
  between operations  14.8 us (2%)
    unnamed x6, waiting for transfers between devices  203 us
    all_gather x1, waiting for transfers between devices, local(): qkv_full = lax.all_gather(w_qkv, 'seq', axis=1, tiled=True)  54.4 us
    all_to_all x1, blocking collectives, to_timesteps(): return lax.all_to_all(values, 'tp', split_axis=1, concat_axis=0, tiled=True)  39.1 us
    all_to_all x1, waiting for transfers between devices, local(): lax.all_to_all(jnp.stack(columns), 'seq', split_axis=1, concat_axis=2, ti...  30.5 us
    gather x4, local copies, waits for them, and re-layouts, local(): jnp.take(table, tokens, axis=0)  24.7 us
    all_to_all x2, waiting for transfers between devices, to_codebooks(): return lax.all_to_all(values, 'tp', split_axis=0, concat_axis=1, tiled=True)  21 us
    dot_general x1, matrix products, local(): jnp.einsum('ctj,cjd->td', d_hidden, w_in, preferred_element_type=jnp.floa...  17.3 us
    dot_general x1, matrix products, local(): jnp.einsum('td,cjd->ctj', normed, w_in, preferred_element_type=jnp.float32)  17.3 us
  transfers between devices with their start and end apart: 12, of which 7 were waited for; matrix products, arithmetic and copies ran while one was open for 36% of the time, Pallas kernels for 0%

profile of v2, /device:TPU:11, one launch (start us, length us, event | category | flops | bytes accessed | tf_op | source)
XLA Modules:
  0.0 719.7 jit_solution(16869381971308041811)
XLA Ops:
  11.1 4.8 copy.167
  16.0 6.2 gather_fusion.2
  22.2 6.2 gather_fusion.3
  28.4 6.2 gather_fusion.4
  34.6 6.2 gather_fusion.1
  40.8 8.6 %gather_fusion = bf16[2048,64]{1,0:T(8,128)(2,1)S(1)} fusion(bf16[16000,64]{1,0:T(8,128)(2,1)} %copy.167, s32[2048]{0:T(1024)S(1)} %fusion.38), kind=kCustom, calls=%fused_computation.4 | custom fusion | bytes 532480 | tf_op jit(solution)/shard_map/jit(_take)/gather | solution.py:65
  52.3 9.8 %copy.239 = bf16[4,2048,64]{2,0,1:T(4,128)(2,1)S(1)} copy(bf16[4,2048,64]{2,1,0:T(8,128)(2,1)S(1)} %pad_maximum_fusion.1) | data formatting | bytes 2097152 | tf_op jit(solution)/shard_map/stack | solution.py:73
  64.3 6.4 all-to-all-start
  70.8 3.7 all-gather
  76.7 30.5 %all-to-all-done = bf16[16,2,16384]{2,1,0:T(2,128)(2,1)S(1)} async-done(((bf16[16,2,16384]{2,1,0:T(2,128)(2,1)}), bf16[16,2,16384]{2,1,0:T(2,128)(2,1)S(1)}, u32[]{:S(2)}, u32[]{:S(2)}) %all-to-all-start) | async-done | bytes 1048608 | tf_op jit(solution)/shard_map/all_to_all | solution.py:73
  112.9 17.3 %multiply_reduce_fusion.2 = (f32[4,128]{1,0:T(4,128)S(1)}, f32[4,128,1024]{2,1,0:T(8,128)S(1)}) fusion(f32[4,128,1024]{2,1,0:T(8,128)} %copy.175, bf16[4,1024,4096]{2,1,0:T(8,128)(2,1)} %param.15, bf16[128,4096]{1,0:T(8,128)(2,1)S(1)} %copy-done.9, f32[4096]{0:T(1024)S(1)} %mul.153, f32[128]{0:T(128)S(1)} %get-tuple-element.41), kind=kOutput, calls=%fused_computation.41 | convolution fusion | flops 4298636800 | bytes 38816256 | tf_op jit(solution)/shard_map/td,cjd->ctj/dot_general | solution.py:74
  130.4 54.4 %all-gather.8.cloned.1.call-done = bf16[4,3072,1024]{2,1,0:T(8,128)(2,1)} async-done(((bf16[4,192,1024]{2,1,0:T(8,128)(2,1)}), bf16[4,3072,1024]{2,1,0:T(8,128)(2,1)}) %all-gather.8.cloned.1.call-update) | async-done | bytes 25165840 | tf_op jit(solution)/shard_map/all_gather | solution.py:80
  184.8 14.2 %convolution_convert_fusion = bf16[4,128,3072]{2,1,0:T(8,128)(2,1)} fusion(bf16[4,128,1024]{2,1,0:T(8,128)(2,1)S(1)} %multiply_convert_fusion.2, bf16[4,3072,1024]{2,1,0:T(8,128)(2,1)} %all-gather.8.cloned.1.call-done), kind=kOutput, calls=%fused_computation.10 | convolution fusion | flops 3222798336 | bytes 29360128 | tf_op jit(solution)/shard_map/ctm,cjm->ctj/dot_general | solution.py:81
  199.1 4.3 copy.176
  203.5 39.1 %all_to_all.106 = bf16[4,128,3072]{2,0,1:T(4,128)(2,1)S(1)} all-to-all(bf16[4,128,3072]{2,0,1:T(4,128)(2,1)S(1)} %copy.176), channel_id=1, replica_groups=mesh['seq'=16,'tp'=2] {'tp'}, dimensions={1} | all-to-all | bytes 6291456 | tf_op jit(solution)/shard_map/all_to_all | solution.py:33
  245.4 8.6 %reshape.82 = bf16[8,64,3,16,64]{4,3,2,1,0:T(8,128)(2,1)} reshape(bf16[8,64,3072]{2,1,0:T(8,128)(2,1)} %bitcast.144) | data formatting | bytes 6291456 | tf_op jit(solution)/shard_map/reshape | solution.py:93
  254.0 4.5 fusion.45
  261.1 15.9 %fusion.46 = (f32[64,16,8]{2,1,0:T(8,128)S(1)}, f32[64,16,8,8]{2,3,1,0:T(8,128)S(1)}) fusion(f32[64,16,8,8]{2,3,1,0:T(8,128)S(1)} %fusion.13, pred[8,8]{0,1:T(8,128)(4,1)S(1)} %iota_compare_fusion), kind=kOutput, calls=%fused_computation.110 | output fusion | flops 393223 | bytes 557120 | tf_op jit(solution)/shard_map/sub | solution.py:28
  280.9 4.3 reshape.83
  285.2 4.4 all-to-all-start.2
  289.6 7.4 %fusion.18 = bf16[4,128,1024]{1,2,0:T(8,128)(2,1)} fusion(bf16[4,1024,1024]{2,1,0:T(8,128)(2,1)} %all-gather.10.cloned.1.call-done, bf16[4,128,1024]{2,1,0:T(8,128)(2,1)S(1)} %copy-done.5), kind=kOutput, calls=%fused_computation.50 | convolution fusion | flops 1074266112 | bytes 10485760 | tf_op jit(solution)/shard_map/ctj,cji->cti/dot_general | solution.py:86
  297.0 2.6 copy.188
  302.1 4.6 all-to-all-start.4
  308.0 10.2 %all-to-all-done.4 = bf16[4,128,1024]{2,0,1:T(4,128)(2,1)} async-done(((bf16[4,128,1024]{2,0,1:T(4,128)(2,1)}), bf16[4,128,1024]{2,0,1:T(4,128)(2,1)}, u32[]{:S(2)}, u32[]{:S(2)}) %all-to-all-start.4) | async-done | bytes 1048608 | tf_op jit(solution)/shard_map/all_to_all | solution.py:33
  320.8 4.0 reshape.85
  324.8 6.6 convert_bitcast_fusion.1
  332.2 3.5 multiply_reduce_fusion
  340.1 4.6 fusion.17
  346.5 3.6 copy.194
  350.1 8.7 %convert_element_type.104 = bf16[8,64,3072]{2,1,0:T(8,128)(2,1)} reshape(bf16[8,64,3,16,64]{4,3,2,1,0:T(8,128)(2,1)} %copy.194) | data formatting | bytes 6291456 | tf_op jit(solution)/shard_map/convert_element_type | solution.py:129
  358.8 5.5 all-to-all-start.5
  364.3 3.6 fusion.47
  367.9 4.1 convert_bitcast_fusion
  372.0 8.6 %copy.186 = bf16[2,8,4,64,1024]{4,3,1,2,0:T(8,128)(2,1)} copy(bf16[2,8,4,64,1024]{4,3,0,1,2:T(8,128)(2,1)} %convert_bitcast_fusion) | data formatting | bytes 16777216 | tf_op jit(solution)/shard_map/convert_element_type | solution.py:113
  380.6 18.5 %all-to-all-done.5 = bf16[8,64,3072]{2,1,0:T(8,128)(2,1)} async-done(((bf16[8,64,3072]{2,1,0:T(8,128)(2,1)}), bf16[8,64,3072]{2,1,0:T(8,128)(2,1)}, u32[]{:S(2)}, u32[]{:S(2)}) %all-to-all-start.5) | async-done | bytes 3145760 | tf_op jit(solution)/shard_map/all_to_all | solution.py:37
  399.1 9.3 %all-to-all-start.3 = ((bf16[2,8,4,64,1024]{4,3,1,2,0:T(8,128)(2,1)}), bf16[2,8,4,64,1024]{4,3,1,2,0:T(8,128)(2,1)}, u32[]{:S(2)}, u32[]{:S(2)}) async-start(bf16[2,8,4,64,1024]{4,3,1,2,0:T(8,128)(2,1)} %copy.186), calls=%async_computation.3 | async-start | bytes 16777216 | tf_op jit(solution)/shard_map/all_to_all | solution.py:114
  408.4 3.8 copy.195
  412.2 14.1 %multiply_reduce_fusion.1 = (f32[4,128]{1,0:T(4,128)S(1)}, f32[4,128,1024]{2,1,0:T(8,128)}) fusion(f32[4,128,1024]{2,1,0:T(8,128)S(1)} %get-tuple-element.43, f32[1024]{0:T(1024)S(1)} %convert_element_type.91, bf16[4,128,3072]{2,1,0:T(8,128)(2,1)} %bitcast.139, bf16[4,3072,1024]{2,1,0:T(8,128)(2,1)} %all-gather.8.cloned.1.call-done), kind=kOutput, calls=%fused_computation.33 | convolution fusion | flops 3222797824 | bytes 32512000 | tf_op jit(solution)/shard_map/ctj,cjm->ctm/dot_general | solution.py:136
  426.3 17.3 %fusion.1 = bf16[128,4096]{1,0:T(8,128)(2,1)} fusion(bf16[4,1024,4096]{2,1,0:T(8,128)(2,1)} %param.15, f32[4,128,1024]{2,1,0:T(8,128)S(1)} %get-tuple-element.43, bf16[4,128,1024]{2,1,0:T(8,128)(2,1)S(1)} %copy-done.6, f32[4,128,1024]{2,1,0:T(8,128)} %get-tuple-element.49, f32[4,128]{1,0:T(4,128)S(1)} %broadcast_multiply_fusion, ...), kind=kOutput, calls=%fused_computation.9 | convolution fusion | flops 4299685888 | bytes 39856128 | tf_op jit(solution)/shard_map/ctj,cjd->td/dot_general | solution.py:143
  445.9 4.4 all-to-all-start.6
  450.3 6.0 copy.197
  456.3 7.9 %all-to-all-done.6 = bf16[128,2,2048]{2,0,1:T(8,128)(2,1)} async-done(((bf16[128,2,2048]{2,0,1:T(8,128)(2,1)}), bf16[128,2,2048]{2,0,1:T(8,128)(2,1)}, u32[]{:S(2)}, u32[]{:S(2)}) %all-to-all-start.6) | async-done | bytes 1048608 | tf_op jit(solution)/shard_map/all_to_all | solution.py:146
  464.1 5.6 all-to-all-start.7
  470.0 9.1 %reduce_sum.78 = bf16[8,4,64,1024]{3,2,0,1:T(8,128)(2,1)} reduce(bf16[2,8,4,64,1024]{4,3,1,2,0:T(8,128)(2,1)} %all-to-all-done.3, bf16[]{:T(256)} %constant.94.clone.1), dimensions={0}, to_apply=%region_4.6 | reduce | flops 2097152 | bytes 12582914 | tf_op jit(solution)/shard_map/reduce_sum | solution.py:117
  480.4 201.1 %all-reduce.3.cloned.1.call-done = bf16[8,4,64,1024]{3,2,0,1:T(8,128)(2,1)} async-done(((bf16[8,4,64,1024]{3,2,0,1:T(8,128)(2,1)}), bf16[8,4,64,1024]{3,2,0,1:T(8,128)(2,1)}) %all-reduce.3.cloned.1.call-update) | async-done | bytes 4194320
  684.0 7.3 %add_convert_fusion = bf16[4,128,1024]{2,1,0:T(8,128)(2,1)} fusion(f32[4,128,1024]{2,1,0:T(8,128)S(1)} %get-tuple-element.43, bf16[4,128,1024]{2,1,0:T(8,128)(2,1)S(1)} %bitcast.142, bf16[4,1024,1024]{2,1,0:T(8,128)(2,1)} %all-gather.10.cloned.1.call-done), kind=kOutput, calls=%fused_computation.35 | convolution fusion | flops 1074790400 | bytes 12582912 | tf_op jit(solution)/shard_map/ctm,cjm->ctj/dot_general | solution.py:103
  693.1 3.8 psum.7
  700.5 11.1 %fusion.3 = f32[4,192,1024]{2,1,0:T(8,128)} fusion(bf16[4,2048,1024]{2,1,0:T(8,128)(2,1)} %all-gather.12.cloned.1.call-done, bf16[4,16,24,8,128]{4,3,2,1,0:T(8,128)(2,1)S(1)} %bitcast.145), kind=kOutput, calls=%fused_computation.18 | convolution fusion | flops 3221225472 | bytes 23068672 | tf_op jit(solution)/shard_map/ctj,cti->cji/dot_general | solution.py:133
  (118 shorter events, 52.4 us)
Async XLA Ops:
  7.2 67.4 %all-gather.6.cloned.1.call-start = ((), (), s32[]{:S(2)}) async-start(), calls=%async_computation.8 | async-start | bytes 1572864 | tf_op jit(solution)/shard_map/all_gather | solution.py:58
  7.9 176.9 %all-gather.8.cloned.1.call-start = ((), (), s32[]{:S(2)}) async-start(), calls=%async_computation.9 | async-start | bytes 26738688 | tf_op jit(solution)/shard_map/all_gather | solution.py:80
  11.1 4.8 copy-start.17
  34.6 6.2 copy-start.14
  62.1 8.7 %copy-start.15 = (bf16[2048]{0:T(1024)(128)(2,1)S(1)}, bf16[2048]{0:T(1024)(128)(2,1)}, u32[]{:S(2)}) copy-start(bf16[2048]{0:T(1024)(128)(2,1)} %param.14) | copy-start | bytes 12292
  62.1 12.5 %copy-start.18 = (bf16[1024]{0:T(1024)(128)(2,1)S(1)}, bf16[1024]{0:T(1024)(128)(2,1)}, u32[]{:S(2)}) copy-start(bf16[1024]{0:T(1024)(128)(2,1)} %param.16) | copy-start | bytes 6148
  64.3 42.8 %all-to-all-start = ((bf16[16,2,16384]{2,1,0:T(2,128)(2,1)}), bf16[16,2,16384]{2,1,0:T(2,128)(2,1)S(1)}, u32[]{:S(2)}, u32[]{:S(2)}) async-start(bf16[16,2,16384]{2,1,0:T(2,128)(2,1)} %reshape.154), calls=%async_computation | async-start | bytes 2097152 | tf_op jit(solution)/shard_map/all_to_all | solution.py:73
  70.8 218.9 %all-gather.10.cloned.1.call-start = ((), (), s32[]{:S(2)}) async-start(), calls=%async_computation.10 | async-start | bytes 8912896 | tf_op jit(solution)/shard_map/all_gather | solution.py:85
  111.0 1.8 copy-start.9
  130.4 68.7 %copy-start = (bf16[4,128,1024]{2,1,0:T(8,128)(2,1)}, bf16[4,128,1024]{2,1,0:T(8,128)(2,1)S(1)}, u32[]{:S(2)}) copy-start(bf16[4,128,1024]{2,1,0:T(8,128)(2,1)S(1)} %multiply_convert_fusion.2) | copy-start | bytes 3145732
  199.1 213.1 %all-gather.12.cloned.1.call-start = ((), (), s32[]{:S(2)}) async-start(), calls=%async_computation.11 | async-start | bytes 17825792 | tf_op jit(solution)/shard_map/all_gather | solution.py:91
  258.6 2.5 copy-start.1
  258.6 2.5 copy-start.3
  258.6 18.5 %copy-start.12 = (bf16[8,64,1,16,64]{4,3,2,1,0:T(8,128)(2,1)}, bf16[8,64,1,16,64]{4,3,2,1,0:T(8,128)(2,1)S(1)}, u32[]{:S(2)}) copy-start(bf16[8,64,1,16,64]{4,3,2,1,0:T(8,128)(2,1)S(1)} %get-tuple-element.25) | copy-start | bytes 3145732
  277.0 2.0 copy-start.21
  277.1 2.2 copy-start.24
  280.9 8.7 %copy-start.5 = (bf16[4,128,1024]{2,1,0:T(8,128)(2,1)S(1)}, bf16[4,128,1024]{2,1,0:T(8,128)(2,1)}, u32[]{:S(2)}) copy-start(bf16[4,128,1024]{2,1,0:T(8,128)(2,1)} %param.23) | copy-start | bytes 3145732
  285.2 16.9 %all-to-all-start.2 = ((bf16[8,64,1024]{2,1,0:T(8,128)(2,1)}), bf16[8,64,1024]{2,1,0:T(8,128)(2,1)}, u32[]{:S(2)}, u32[]{:S(2)}) async-start(bf16[8,64,1024]{2,1,0:T(8,128)(2,1)} %reshape.83), calls=%async_computation.2 | async-start | bytes 2097152 | tf_op jit(solution)/shard_map/all_to_all | solution.py:37
  302.1 16.1 %all-to-all-start.4 = ((bf16[4,128,1024]{2,0,1:T(4,128)(2,1)}), bf16[4,128,1024]{2,0,1:T(4,128)(2,1)}, u32[]{:S(2)}, u32[]{:S(2)}) async-start(bf16[4,128,1024]{2,0,1:T(4,128)(2,1)} %copy.188), calls=%async_computation.4 | async-start | bytes 2097152 | tf_op jit(solution)/shard_map/all_to_all | solution.py:33
  324.8 6.6 copy-start.10
  324.8 6.6 copy-start.13
  324.8 7.3 %copy-start.22 = (f32[64,16,8,8]{2,3,1,0:T(8,128)S(1)}, f32[64,16,8,8]{2,3,1,0:T(8,128)}, u32[]{:S(2)}) copy-start(f32[64,16,8,8]{2,3,1,0:T(8,128)} %copy-done.21) | copy-start | bytes 786436
  324.8 7.3 %copy-start.25 = (f32[64,16,8]{2,1,0:T(8,128)S(1)}, f32[64,16,8]{2,1,0:T(8,128)}, u32[]{:S(2)}) copy-start(f32[64,16,8]{2,1,0:T(8,128)} %copy-done.24) | copy-start | bytes 98308
  332.2 5.6 copy-start.4
  335.7 2.0 copy-start.23
  337.7 2.3 copy-start.2
  358.8 40.3 %all-to-all-start.5 = ((bf16[8,64,3072]{2,1,0:T(8,128)(2,1)}), bf16[8,64,3072]{2,1,0:T(8,128)(2,1)}, u32[]{:S(2)}, u32[]{:S(2)}) async-start(bf16[8,64,3072]{2,1,0:T(8,128)(2,1)} %convert_element_type.104), calls=%async_computation.5 | async-start | bytes 6291456 | tf_op jit(solution)/shard_map/all_to_all | solution.py:37
  399.1 46.8 %all-to-all-start.3 = ((bf16[2,8,4,64,1024]{4,3,1,2,0:T(8,128)(2,1)}), bf16[2,8,4,64,1024]{4,3,1,2,0:T(8,128)(2,1)}, u32[]{:S(2)}, u32[]{:S(2)}) async-start(bf16[2,8,4,64,1024]{4,3,1,2,0:T(8,128)(2,1)} %copy.186), calls=%async_computation.3 | async-start | bytes 16777216 | tf_op jit(solution)/shard_map/all_to_all | solution.py:114
  412.2 14.1 %copy-start.6 = (bf16[4,128,1024]{2,1,0:T(8,128)(2,1)S(1)}, bf16[4,128,1024]{2,1,0:T(8,128)(2,1)}, u32[]{:S(2)}) copy-start(bf16[4,128,1024]{2,1,0:T(8,128)(2,1)} %param.23) | copy-start | bytes 3145732
  445.9 18.3 %all-to-all-start.6 = ((bf16[128,2,2048]{2,0,1:T(8,128)(2,1)}), bf16[128,2,2048]{2,0,1:T(8,128)(2,1)}, u32[]{:S(2)}, u32[]{:S(2)}) async-start(bf16[128,2,2048]{2,0,1:T(8,128)(2,1)} %bitcast.152), calls=%async_computation.6 | async-start | bytes 2097152 | tf_op jit(solution)/shard_map/all_to_all | solution.py:146
  464.1 234.0 %all-to-all-start.7 = ((bf16[4,128,3072]{1,0,2:T(4,128)(2,1)}), bf16[4,128,3072]{1,0,2:T(4,128)(2,1)}, u32[]{:S(2)}, u32[]{:S(2)}) async-start(bf16[4,128,3072]{1,0,2:T(4,128)(2,1)} %copy.197), calls=%async_computation.7 | async-start | bytes 6291456 | tf_op jit(solution)/shard_map/all_to_all | solution.py:132
  469.8 211.7 %all-reduce.3.cloned.1.call-start = ((), (), s32[]{:S(2)}) async-start(), calls=%async_computation.12 | async-start | bytes 8388608
  479.1 0.7 copy-start.16
  479.1 0.7 copy-start.20
  684.0 8.9 %copy-start.7 = (bf16[128,2048]{1,0:T(8,128)(2,1)S(1)}, bf16[128,2048]{1,0:T(8,128)(2,1)}, u32[]{:S(2)}) copy-start(bf16[128,2048]{1,0:T(8,128)(2,1)} %param.13) | copy-start | bytes 1572868
  691.3 5.6 copy-start.8
  691.3 5.6 copy-start.19
  700.5 11.1 %copy-start.11 = (bf16[4,64,1024]{2,1,0:T(8,128)(2,1)S(1)}, bf16[4,64,1024]{2,1,0:T(8,128)(2,1)}, u32[]{:S(2)}) copy-start(bf16[4,64,1024]{2,1,0:T(8,128)(2,1)} %dynamic-slice_bitcast_fusion) | copy-start | bytes 1572868
Sparse Core Ops, SparseCore 0:
  9.5 22.4 all-gather.5
  33.6 151.2 all-gather.7
  199.2 72.7 all-gather.9
  274.0 123.8 all-gather.11
  479.3 202.1 all-reduce.2

commit v3 on v1

--- a/solution.py
+++ b/solution.py
@@ -106,9 +106,6 @@
     out_terms = jnp.einsum("ctm,cjm->ctj", attended, out_full, preferred_element_type=jnp.float32)
     depth_out = (hidden + out_terms).astype(jnp.bfloat16)
     attended_all = lax.all_gather(attended, "seq", axis=1, tiled=True)
-    out_grad = jnp.einsum(
-        "ctj,cti->cji", cot_columns, attended_all, preferred_element_type=jnp.float32
-    )
     d_time = to_timesteps(d_attended).reshape(books, steps_here, HEADS, HEAD_DIM)
     d_weights = jnp.einsum("ithd,jthd->thij", d_time, values, preferred_element_type=jnp.float32)
     d_values = jnp.einsum(
@@ -132,13 +129,21 @@
     )
     d_hidden = d_hidden.astype(jnp.bfloat16)
     d_partial = jnp.einsum("ctj,cjd->td", d_hidden, w_in, preferred_element_type=jnp.float32)
-    d_features = lax.psum_scatter(
-        d_partial.astype(jnp.bfloat16), "tp", scatter_dimension=1, tiled=True
-    ).astype(jnp.float32)
+    sides = lax.axis_size("tp")
+    d_pieces = d_partial.astype(jnp.bfloat16).reshape(trunk.shape[0], sides, -1)
+    d_pieces = lax.all_to_all(d_pieces, "tp", split_axis=1, concat_axis=1, tiled=True)
+    d_features = jnp.sum(d_pieces.astype(jnp.float32), axis=1)
     trunk_gained = gain_local * d_features
     row_total = lax.psum(jnp.sum(trunk_float * trunk_gained, axis=1, keepdims=True), "tp")
     trunk_grad = row_scale * trunk_gained - trunk_float * row_scale**3 * row_total / model_width
-    return (depth_out, trunk_grad.astype(jnp.bfloat16), qkv_grad, out_grad)
+    trunk_grad = trunk_grad.astype(jnp.bfloat16)
+    attended_all, trunk_grad, qkv_grad = lax.optimization_barrier(
+        (attended_all, trunk_grad, qkv_grad)
+    )
+    out_grad = jnp.einsum(
+        "ctj,cti->cji", cot_columns, attended_all, preferred_element_type=jnp.float32
+    )
+    return (depth_out, trunk_grad, qkv_grad, out_grad)
 
 
 def solution(mesh):

time: 669 us -> 652 us (0.975)
  waiting for transfers between devices: 199 us -> 176 us
    all_gather x1, waiting for transfers between devices: 119 us -> 0.01 us  [local(): attended_all = lax.all_gather(attended, 'seq', axis=1, tiled=True)]
    all_to_all x1, waiting for transfers between devices: 0.01 us -> 109 us  [local(): lax.all_to_all(d_projected, 'seq', split_axis=2, concat_axis=1, tiled=True)]
    reduce_scatter x1 -> x0, waiting for transfers between devices: 16.9 us -> none  [local(): lax.psum_scatter(d_partial.astype(jnp.bfloat16), 'tp', scatter_dimension=...]
  transfers between devices with their start and end apart: 8 -> 8, of which waited for: 4 -> 4; matrix products, arithmetic and copies ran while one was open for 37% -> 38% of each run, Pallas kernels for 0% -> 0%
where the time goes in v3:
time: 652 us; the launch traced here: 643 us
  waiting for transfers between devices  176 us (27%)
  blocking collectives  159 us (24%)
  matrix products  124 us (19%)
  local copies, waits for them, and re-layouts  121 us (19%)
  other arithmetic  26.6 us (4%)
  starting transfers between devices  20.5 us (3%)
  between operations  14.8 us (2%)
    all_to_all x1, waiting for transfers between devices, local(): lax.all_to_all(d_projected, 'seq', split_axis=2, concat_axis=1, tiled=True)  109 us
    all_to_all x2, blocking collectives, to_timesteps(): return lax.all_to_all(values, 'tp', split_axis=1, concat_axis=0, tiled=True)  54.6 us
    all_to_all x2, blocking collectives, to_codebooks(): return lax.all_to_all(values, 'tp', split_axis=0, concat_axis=1, tiled=True)  53.2 us
    all_to_all x1, blocking collectives, local(): lax.all_to_all(cot_here, 'seq', split_axis=2, concat_axis=1, tiled=True)  43.5 us
    all_to_all x1, waiting for transfers between devices, local(): lax.all_to_all(jnp.stack(columns), 'seq', split_axis=1, concat_axis=2, ti...  31.1 us
    all_gather x1, waiting for transfers between devices, local(): qkv_full = lax.all_gather(w_qkv, 'seq', axis=1, tiled=True)  30.6 us
    gather x4, local copies, waits for them, and re-layouts, local(): jnp.take(table, tokens, axis=0)  24.7 us
    dot_general x1, matrix products, local(): jnp.einsum('ctj,cjd->td', d_hidden, w_in, preferred_element_type=jnp.floa...  17.4 us
  transfers between devices with their start and end apart: 8, of which 4 were waited for; matrix products, arithmetic and copies ran while one was open for 38% of the time, Pallas kernels for 0%

profile of v3, /device:TPU:11, one launch (start us, length us, event | category | flops | bytes accessed | tf_op | source)
XLA Modules:
  0.0 642.7 jit_solution(5239480992229073325)
XLA Ops:
  10.2 4.9 copy.135
  16.0 6.2 gather_fusion.1
  22.2 8.3 %gather_fusion = bf16[2048,64]{1,0:T(8,128)(2,1)S(1)} fusion(bf16[16000,64]{1,0:T(8,128)(2,1)} %copy.135, s32[2048]{0:T(1024)S(1)} %fusion.38), kind=kCustom, calls=%fused_computation.4 | custom fusion | bytes 532480 | tf_op jit(solution)/shard_map/jit(_take)/gather | solution.py:65
  30.5 6.2 gather_fusion.2
  36.7 6.2 gather_fusion.3
  42.9 6.2 gather_fusion.4
  49.2 2.2 fusion.37
  52.0 9.8 %copy.207 = bf16[4,2048,64]{2,0,1:T(4,128)(2,1)S(1)} copy(bf16[4,2048,64]{2,1,0:T(8,128)(2,1)S(1)} %pad_maximum_fusion.1) | data formatting | bytes 2097152 | tf_op jit(solution)/shard_map/stack | solution.py:73
  61.8 2.2 reshape.145
  64.0 6.6 %all-to-all-start = ((bf16[16,2,16384]{2,1,0:T(2,128)(2,1)}), bf16[16,2,16384]{2,1,0:T(2,128)(2,1)S(1)}, u32[]{:S(2)}, u32[]{:S(2)}) async-start(bf16[16,2,16384]{2,1,0:T(2,128)(2,1)} %reshape.145), calls=%async_computation | async-start | bytes 2097152 | tf_op jit(solution)/shard_map/all_to_all | solution.py:73
  70.6 3.7 all-gather
  75.9 31.1 %all-to-all-done = bf16[16,2,16384]{2,1,0:T(2,128)(2,1)S(1)} async-done(((bf16[16,2,16384]{2,1,0:T(2,128)(2,1)}), bf16[16,2,16384]{2,1,0:T(2,128)(2,1)S(1)}, u32[]{:S(2)}, u32[]{:S(2)}) %all-to-all-start) | async-done | bytes 1048608 | tf_op jit(solution)/shard_map/all_to_all | solution.py:73
  112.7 17.2 %multiply_reduce_fusion.2 = (f32[4,128]{1,0:T(4,128)S(1)}, f32[4,128,1024]{2,1,0:T(8,128)S(1)}) fusion(f32[4,128,1024]{2,1,0:T(8,128)} %copy.143, bf16[4,1024,4096]{2,1,0:T(8,128)(2,1)} %param.15, bf16[128,4096]{1,0:T(8,128)(2,1)S(1)} %copy-done.8, f32[4096]{0:T(1024)S(1)} %mul.153, f32[128]{0:T(128)S(1)} %get-tuple-element.49), kind=kOutput, calls=%fused_computation.40 | convolution fusion | flops 4298636800 | bytes 38816256 | tf_op jit(solution)/shard_map/td,cjd->ctj/dot_general | solution.py:74
  132.8 43.5 %all_to_all.119 = bf16[4,128,1024]{1,0,2:T(4,128)(2,1)S(1)} all-to-all(bf16[4,128,1024]{1,0,2:T(4,128)(2,1)} %copy.144), channel_id=1, replica_groups=mesh['seq'=16,'tp'=2] {'seq'}, dimensions={2} | all-to-all | bytes 2097152 | tf_op jit(solution)/shard_map/all_to_all | solution.py:82
  176.7 30.6 %all-gather.9.cloned.1.call-done = bf16[4,3072,1024]{2,1,0:T(8,128)(2,1)} async-done(((bf16[4,192,1024]{2,1,0:T(8,128)(2,1)}), bf16[4,3072,1024]{2,1,0:T(8,128)(2,1)}) %all-gather.9.cloned.1.call-update) | async-done | bytes 25165840 | tf_op jit(solution)/shard_map/all_gather | solution.py:80
  207.3 14.6 %convolution_convert_fusion = bf16[4,128,3072]{2,1,0:T(8,128)(2,1)} fusion(bf16[4,128,1024]{2,1,0:T(8,128)(2,1)} %multiply_convert_fusion.2, bf16[4,3072,1024]{2,1,0:T(8,128)(2,1)} %all-gather.9.cloned.1.call-done), kind=kOutput, calls=%fused_computation.9 | convolution fusion | flops 3222798336 | bytes 29360128 | tf_op jit(solution)/shard_map/ctm,cjm->ctj/dot_general | solution.py:84
  222.0 4.3 copy.147
  226.3 39.1 %all_to_all.120 = bf16[4,128,3072]{2,0,1:T(4,128)(2,1)S(1)} all-to-all(bf16[4,128,3072]{2,0,1:T(4,128)(2,1)S(1)} %copy.147), channel_id=1, replica_groups=mesh['seq'=16,'tp'=2] {'tp'}, dimensions={1} | all-to-all | bytes 6291456 | tf_op jit(solution)/shard_map/all_to_all | solution.py:33
  268.3 8.6 %reshape.79 = bf16[8,64,3,16,64]{4,3,2,1,0:T(8,128)(2,1)} reshape(bf16[8,64,3072]{2,1,0:T(8,128)(2,1)} %bitcast.135) | data formatting | bytes 6291456 | tf_op jit(solution)/shard_map/reshape | solution.py:96
  276.9 4.5 fusion.45
  281.4 2.5 fusion.13
  284.0 15.9 %fusion.46 = (f32[64,16,8]{2,1,0:T(8,128)S(1)}, f32[64,16,8,8]{2,3,1,0:T(8,128)S(1)}) fusion(f32[64,16,8,8]{2,3,1,0:T(8,128)S(1)} %fusion.13, pred[8,8]{0,1:T(8,128)(4,1)S(1)} %iota_compare_fusion), kind=kOutput, calls=%fused_computation.109 | output fusion | flops 393223 | bytes 557120 | tf_op jit(solution)/shard_map/sub | solution.py:28
  303.7 4.2 reshape.80
  308.0 16.2 %all_to_all.121 = bf16[8,64,1024]{2,1,0:T(8,128)(2,1)S(1)} all-to-all(bf16[8,64,1024]{2,1,0:T(8,128)(2,1)} %reshape.80), channel_id=1, replica_groups=mesh['seq'=16,'tp'=2] {'tp'}, dimensions={0} | all-to-all | bytes 2097152 | tf_op jit(solution)/shard_map/all_to_all | solution.py:37
  325.4 7.6 %fusion.18 = bf16[4,128,1024]{1,2,0:T(8,128)(2,1)} fusion(bf16[4,1024,1024]{2,1,0:T(8,128)(2,1)} %all-gather.11.cloned.1.call-done, bf16[4,128,1024]{2,1,0:T(8,128)(2,1)} %param.23), kind=kOutput, calls=%fused_computation.49 | convolution fusion | flops 1074266112 | bytes 10485760 | tf_op jit(solution)/shard_map/ctj,cji->cti/dot_general | solution.py:89
  332.9 2.6 copy.156
  335.6 15.5 %all_to_all.122 = bf16[4,128,1024]{2,0,1:T(4,128)(2,1)S(1)} all-to-all(bf16[4,128,1024]{2,0,1:T(4,128)(2,1)} %copy.156), channel_id=1, replica_groups=mesh['seq'=16,'tp'=2] {'tp'}, dimensions={1} | all-to-all | bytes 2097152 | tf_op jit(solution)/shard_map/all_to_all | solution.py:33
  352.5 4.0 reshape.81
  356.5 4.9 convert_bitcast_fusion
  362.1 4.9 multiply_reduce_fusion
  367.1 4.7 fusion.17
  371.8 4.9 fusion.16
  378.5 3.7 copy.162
  382.2 8.7 %convert_element_type.91 = bf16[8,64,3072]{2,1,0:T(8,128)(2,1)} reshape(bf16[8,64,3,16,64]{4,3,2,1,0:T(8,128)(2,1)} %copy.162) | data formatting | bytes 6291456 | tf_op jit(solution)/shard_map/convert_element_type | solution.py:117
  390.9 37.1 %all_to_all.123 = bf16[8,64,3072]{2,1,0:T(8,128)(2,1)S(1)} all-to-all(bf16[8,64,3072]{2,1,0:T(8,128)(2,1)} %convert_element_type.91), channel_id=1, replica_groups=mesh['seq'=16,'tp'=2] {'tp'}, dimensions={0} | all-to-all | bytes 6291456 | tf_op jit(solution)/shard_map/all_to_all | solution.py:37
  429.9 15.2 %multiply_reduce_fusion.1 = (f32[4,128]{1,0:T(4,128)S(1)}, f32[4,128,1024]{2,1,0:T(8,128)}) fusion(f32[4,128,1024]{2,1,0:T(8,128)S(1)} %get-tuple-element.51, f32[1024]{0:T(1024)S(1)} %convert_element_type.80, bf16[4,128,3072]{2,1,0:T(8,128)(2,1)} %bitcast.130, bf16[4,3072,1024]{2,1,0:T(8,128)(2,1)} %all-gather.9.cloned.1.call-done), kind=kOutput, calls=%fused_computation.32 | convolution fusion | flops 3222797824 | bytes 32512000 | tf_op jit(solution)/shard_map/ctj,cjm->ctm/dot_general | solution.py:124
  445.1 17.4 %fusion.1 = bf16[128,4096]{1,0:T(8,128)(2,1)} fusion(bf16[4,1024,4096]{2,1,0:T(8,128)(2,1)} %param.15, f32[4,128,1024]{2,1,0:T(8,128)S(1)} %get-tuple-element.51, bf16[4,128,1024]{2,1,0:T(8,128)(2,1)S(1)} %copy-done.7, f32[4,128,1024]{2,1,0:T(8,128)} %get-tuple-element.57, f32[4,128]{1,0:T(4,128)S(1)} %broadcast_multiply_fusion, ...), kind=kOutput, calls=%fused_computation.8 | convolution fusion | flops 4299685888 | bytes 39856128 | tf_op jit(solution)/shard_map/ctj,cjd->td/dot_general | solution.py:131
  462.5 2.3 copy.206
  464.8 4.4 all-to-all-start.6
  469.3 5.9 copy.165
  475.2 4.5 all-to-all-done.6
  479.7 9.4 %all-to-all-start.7 = ((bf16[4,128,3072]{1,0,2:T(4,128)(2,1)}), bf16[4,128,3072]{1,0,2:T(4,128)(2,1)}, u32[]{:S(2)}, u32[]{:S(2)}) async-start(bf16[4,128,3072]{1,0,2:T(4,128)(2,1)} %copy.165), calls=%async_computation.7 | async-start | bytes 6291456 | tf_op jit(solution)/shard_map/all_to_all | solution.py:120
  489.1 7.7 %add_convert_fusion = bf16[4,128,1024]{2,1,0:T(8,128)(2,1)} fusion(f32[4,128,1024]{2,1,0:T(8,128)S(1)} %get-tuple-element.51, bf16[4,128,1024]{2,1,0:T(8,128)(2,1)} %bitcast.138, bf16[4,1024,1024]{2,1,0:T(8,128)(2,1)} %all-gather.11.cloned.1.call-done), kind=kOutput, calls=%fused_computation.34 | convolution fusion | flops 1074790400 | bytes 12582912 | tf_op jit(solution)/shard_map/ctm,cjm->ctj/dot_general | solution.py:106
  498.6 4.2 psum.7
  504.0 108.6 %all-to-all-done.7 = bf16[4,128,3072]{1,0,2:T(4,128)(2,1)} async-done(((bf16[4,128,3072]{1,0,2:T(4,128)(2,1)}), bf16[4,128,3072]{1,0,2:T(4,128)(2,1)}, u32[]{:S(2)}, u32[]{:S(2)}) %all-to-all-start.7) | async-done | bytes 3145760 | tf_op jit(solution)/shard_map/all_to_all | solution.py:120
  612.6 2.3 copy.166
  614.9 11.1 %fusion.3 = f32[4,192,1024]{2,1,0:T(8,128)} fusion(bf16[4,2048,1024]{2,1,0:T(8,128)(2,1)} %all-gather.15.cloned.1.call-done, bf16[4,16,24,8,128]{4,3,2,1,0:T(8,128)(2,1)S(1)} %bitcast.136), kind=kOutput, calls=%fused_computation.17 | convolution fusion | flops 3221225472 | bytes 23068672 | tf_op jit(solution)/shard_map/ctj,cti->cji/dot_general | solution.py:121
  626.0 9.8 %fusion.47 = f32[4,64,1024]{2,1,0:T(8,128)} fusion(bf16[4,2048,64]{1,2,0:T(8,128)(2,1)S(1)} %bitcast.132, bf16[4,2048,1024]{2,1,0:T(8,128)(2,1)} %all-gather.13.cloned.1.call-done), kind=kOutput, calls=%fused_computation.111 | convolution fusion | flops 1073741824 | bytes 18874368 | tf_op jit(solution)/shard_map/ctj,cti->cji/dot_general | solution.py:143
  (99 shorter events, 31.7 us)
Async XLA Ops:
  7.2 67.2 %all-gather.7.cloned.1.call-start = ((), (), s32[]{:S(2)}) async-start(), calls=%async_computation.8 | async-start | bytes 1572864 | tf_op jit(solution)/shard_map/all_gather | solution.py:58
  7.9 199.4 %all-gather.9.cloned.1.call-start = ((), (), s32[]{:S(2)}) async-start(), calls=%async_computation.9 | async-start | bytes 26738688 | tf_op jit(solution)/shard_map/all_gather | solution.py:80
  10.2 5.7 copy-start.14
  15.4 6.8 %copy-start.12 = (s32[2048]{0:T(1024)S(1)}, s32[2048]{0:T(1024)}, u32[]{:S(2)}) copy-start(s32[2048]{0:T(1024)} %param.21) | copy-start | bytes 24580
  61.8 8.9 %copy-start.13 = (bf16[2048]{0:T(1024)(128)(2,1)S(1)}, bf16[2048]{0:T(1024)(128)(2,1)}, u32[]{:S(2)}) copy-start(bf16[2048]{0:T(1024)(128)(2,1)} %param.14) | copy-start | bytes 12292
  61.8 12.6 %copy-start.15 = (bf16[1024]{0:T(1024)(128)(2,1)S(1)}, bf16[1024]{0:T(1024)(128)(2,1)}, u32[]{:S(2)}) copy-start(bf16[1024]{0:T(1024)(128)(2,1)} %param.16) | copy-start | bytes 6148
  64.0 43.0 %all-to-all-start = ((bf16[16,2,16384]{2,1,0:T(2,128)(2,1)}), bf16[16,2,16384]{2,1,0:T(2,128)(2,1)S(1)}, u32[]{:S(2)}, u32[]{:S(2)}) async-start(bf16[16,2,16384]{2,1,0:T(2,128)(2,1)} %reshape.145), calls=%async_computation | async-start | bytes 2097152 | tf_op jit(solution)/shard_map/all_to_all | solution.py:73
  70.6 254.8 %all-gather.11.cloned.1.call-start = ((), (), s32[]{:S(2)}) async-start(), calls=%async_computation.10 | async-start | bytes 8912896 | tf_op jit(solution)/shard_map/all_gather | solution.py:88
  110.9 1.8 copy-start.8
  130.0 1.4 copy-start.6
  222.0 207.9 %all-gather.15.cloned.1.call-start = ((), (), s32[]{:S(2)}) async-start(), calls=%async_computation.12 | async-start | bytes 17825792 | tf_op jit(solution)/shard_map/all_gather | solution.py:94
  268.3 357.7 %all-gather.13.cloned.1.call-start = ((), (), s32[]{:S(2)}) async-start(), calls=%async_computation.11 | async-start | bytes 17825792 | tf_op jit(solution)/shard_map/all_gather | solution.py:108
  281.4 2.5 copy-start
  281.4 2.5 copy-start.2
  281.4 18.5 %copy-start.10 = (bf16[8,64,1,16,64]{4,3,2,1,0:T(8,128)(2,1)}, bf16[8,64,1,16,64]{4,3,2,1,0:T(8,128)(2,1)S(1)}, u32[]{:S(2)}) copy-start(bf16[8,64,1,16,64]{4,3,2,1,0:T(8,128)(2,1)S(1)} %get-tuple-element.33) | copy-start | bytes 3145732
  299.9 2.0 copy-start.16
  299.9 2.2 copy-start.18
  356.5 4.9 copy-start.9
  356.5 4.9 copy-start.11
  356.5 5.5 copy-start.17
  356.5 5.6 copy-start.19
  362.1 4.9 copy-start.3
  367.1 4.8 copy-start.1
  429.9 15.2 %copy-start.7 = (bf16[4,128,1024]{2,1,0:T(8,128)(2,1)S(1)}, bf16[4,128,1024]{2,1,0:T(8,128)(2,1)}, u32[]{:S(2)}) copy-start(bf16[4,128,1024]{2,1,0:T(8,128)(2,1)} %param.23) | copy-start | bytes 3145732
  464.8 14.8 %all-to-all-start.6 = ((bf16[128,2,2048]{2,0,1:T(8,128)(2,1)}), bf16[128,2,2048]{2,0,1:T(8,128)(2,1)}, u32[]{:S(2)}, u32[]{:S(2)}) async-start(bf16[128,2,2048]{2,0,1:T(8,128)(2,1)} %bitcast.145), calls=%async_computation.6 | async-start | bytes 2097152 | tf_op jit(solution)/shard_map/all_to_all | solution.py:134
  479.7 132.9 %all-to-all-start.7 = ((bf16[4,128,3072]{1,0,2:T(4,128)(2,1)}), bf16[4,128,3072]{1,0,2:T(4,128)(2,1)}, u32[]{:S(2)}, u32[]{:S(2)}) async-start(bf16[4,128,3072]{1,0,2:T(4,128)(2,1)} %copy.165), calls=%async_computation.7 | async-start | bytes 6291456 | tf_op jit(solution)/shard_map/all_to_all | solution.py:120
  489.1 9.2 %copy-start.4 = (bf16[128,2048]{1,0:T(8,128)(2,1)S(1)}, bf16[128,2048]{1,0:T(8,128)(2,1)}, u32[]{:S(2)}) copy-start(bf16[128,2048]{1,0:T(8,128)(2,1)} %param.13) | copy-start | bytes 1572868
  496.7 6.0 copy-start.5
Sparse Core Ops, SparseCore 0:
  9.5 22.4 all-gather.6
  33.6 173.6 all-gather.8
  222.1 72.7 all-gather.10
  297.4 123.8 all-gather.14
  423.3 181.4 all-gather.12
